TPU v7x, 512 devices: a whole 4x8x8 slice. The times are simulated.
512 devices in a mesh: own: 128 (over y, z, core), rep: 4 (over x).
Axes of the slice: x: 4, y: 8, z: 8, core: 2. Of those that a mesh axis runs over, the one named last changes fastest.
Arguments:
- sample_grads: bfloat16 [131072, 1024], P(('own', 'rep')), may hold values from -6 to 6
- send_count: int32 [512, 128], P(('own', 'rep')), may hold values from 1 to 4, as said below
- send_user: int32 [65536, 4], P(('own', 'rep')), may hold values from 0 to 1
- histories: bfloat16 [1024, 256, 1024], P(('own', 'rep')), may hold values from -6 to 6
- hist_len: int32 [1024], P(('own', 'rep')), may hold values from 64 to 256, as said below
- w_in: bfloat16 [1024, 512], replicated, may hold values from -0.1875 to 0.1875
- w_out: bfloat16 [128, 1024], replicated, may hold values from -0.5 to 0.5
Outputs:
- hist_grad: bfloat16 [1024, 256, 1024], P(('own', 'rep'))
- grad_in: float32 [1024, 512], P(('own', 'rep'))
- grad_out: float32 [128, 1024], P(None, ('own', 'rep'))
Inputs may be any that keep to these rules, and one draw needn't show every extreme that they name: `send_count`: within every replica group one owner, drawn anew, receives exactly 4 samples from every device; every other count lies between 1 and 1; a row sums to at most 256. `send_user`: entries at positions c >= the matching send_count are unused. `hist_len`: every device holds one history of length exactly 256.
All inputs are finite; a program needn't handle non-finite values.
Results may differ from a plain program's by a relative error of at most 0.017.
Values may be sent and summed in bfloat16 or wider, within the bound.
A program may use at most 64 MiB of HBM per device.

v0:
```python
import jax
import jax.numpy as jnp
from jax import lax
from jax.sharding import PartitionSpec as P


def encode(x_f, length, wi_f, wo_f):
    seq = x_f.shape[0]
    width = wo_f.shape[0]
    msq = jnp.mean(x_f * x_f, axis=-1, keepdims=True)
    normed = (x_f * lax.rsqrt(msq + 1e-05)).astype(jnp.bfloat16)
    proj = jax.nn.silu(
        jnp.dot(normed, wi_f.astype(jnp.bfloat16), preferred_element_type=jnp.float32)
    )
    gate_u = proj[:, :width]
    values = proj[:, width : 2 * width].astype(jnp.bfloat16)
    query = proj[:, 2 * width : 3 * width].astype(jnp.bfloat16)
    keys = proj[:, 3 * width :].astype(jnp.bfloat16)
    scores = jnp.dot(query, keys.T, preferred_element_type=jnp.float32) * width ** (-0.5)
    rowpos = jnp.arange(seq, dtype=jnp.int32)[:, None]
    colpos = jnp.arange(seq, dtype=jnp.int32)[None, :]
    lenf = length.astype(jnp.float32)
    visible = (colpos <= rowpos) & (colpos < length)
    weights = (jnp.where(visible, jax.nn.silu(scores), 0.0) / lenf).astype(jnp.bfloat16)
    attended = jnp.dot(weights, values, preferred_element_type=jnp.float32)
    mixed = (attended * gate_u).astype(jnp.bfloat16)
    out = x_f + jnp.dot(mixed, wo_f.astype(jnp.bfloat16), preferred_element_type=jnp.float32)
    keep = (jnp.arange(seq, dtype=jnp.int32) < length).astype(jnp.float32)
    return jnp.sum(out * keep[:, None], axis=0) / lenf


def user_backward(history, length, grad, wi_f, wo_f):

    def apply(x_f, wi, wo):
        return encode(x_f, length, wi, wo)

    pooled, pull = jax.vjp(apply, history.astype(jnp.float32), wi_f, wo_f)
    dx, dwi, dwo = pull(grad)
    return (dx.astype(jnp.bfloat16), dwi, dwo)


def body(sample_grads, send_count, send_user, histories, hist_len, w_in, w_out):
    owners = lax.axis_size("own")
    capacity = send_user.shape[1]
    local_users = histories.shape[0]
    sample_rows = sample_grads.shape[0]
    width = sample_grads.shape[1]
    counts = send_count[0]
    offsets = jnp.cumsum(counts) - counts
    position = jnp.arange(capacity, dtype=jnp.int32)
    index = jnp.clip(offsets[:, None] + position[None, :], 0, sample_rows - 1).reshape(-1)
    live = (position[None, :] < counts[:, None]).reshape(-1)
    picked = jnp.where(live[:, None], sample_grads[index], jnp.zeros((), jnp.bfloat16))
    picked = picked.reshape(owners, capacity, width)
    user_ids = jnp.arange(local_users, dtype=jnp.int32)
    arrived, arrived_slots = (
        lax.all_to_all(picked, "own", split_axis=0, concat_axis=0, tiled=True),
        lax.all_to_all(send_user, "own", split_axis=0, concat_axis=0, tiled=True),
    )
    table = (arrived_slots.reshape(-1)[:, None] == user_ids[None, :]).astype(jnp.bfloat16)
    user_grad = jnp.dot(table.T, arrived.reshape(-1, width), preferred_element_type=jnp.float32)
    wi_f = w_in.astype(jnp.float32)
    wo_f = w_out.astype(jnp.float32)

    def each_user(carry, item):
        history, length, grad = item
        dx, dwi, dwo = user_backward(history, length, grad, wi_f, wo_f)
        return ((carry[0] + dwi, carry[1] + dwo), dx)

    init = (jnp.zeros(wi_f.shape, jnp.float32), jnp.zeros(wo_f.shape, jnp.float32))
    sums, hist_grad = lax.scan(each_user, init, (histories, hist_len, user_grad))
    grad_in, grad_out = (
        lax.psum_scatter(sums[0], ("own", "rep"), scatter_dimension=0, tiled=True),
        lax.psum_scatter(sums[1], ("own", "rep"), scatter_dimension=1, tiled=True),
    )
    return (hist_grad, grad_in, grad_out)


def solution(mesh):
    return jax.shard_map(
        body,
        mesh=mesh,
        in_specs=(
            P(("own", "rep"), None),
            P(("own", "rep"), None),
            P(("own", "rep"), None),
            P(("own", "rep"), None, None),
            P(("own", "rep")),
            P(),
            P(),
        ),
        out_specs=(P(("own", "rep"), None, None), P(("own", "rep"), None), P(None, ("own", "rep"))),
        check_vma=False,
    )
```

profile of v0, /device:TPU:1, one launch (start us, length us, event | category | flops | bytes accessed | tf_op | source)
XLA Modules:
  0.0 391.3 jit_solution(4052920270612664455)
XLA Ops:
  7.2 1.5 copy.15
  8.7 18.4 %all-to-all-start = ((s32[128,1,4]{2,1,0:T(1,128)}), s32[128,1,4]{2,1,0:T(1,128)S(1)}, u32[]{:S(2)}, u32[]{:S(2)}) async-start(s32[128,1,4]{2,1,0:T(1,128)} %bitcast), calls=%async_computation | async-start | bytes 131072 | tf_op jit(solution)/shard_map/all_to_all | solution.py:58
  27.1 0.8 copy.16
  28.1 0.7 bitcast_subtract_fusion
  29.0 2.1 gather_fusion
  31.8 1.6 broadcast_select_fusion
  33.4 5.1 %all-to-all-done = s32[128,1,4]{2,1,0:T(1,128)S(1)} async-done(((s32[128,1,4]{2,1,0:T(1,128)}), s32[128,1,4]{2,1,0:T(1,128)S(1)}, u32[]{:S(2)}, u32[]{:S(2)}) %all-to-all-start) | async-done | bytes 2080 | tf_op jit(solution)/shard_map/all_to_all | solution.py:58
  38.5 8.6 %all-to-all-start.1 = ((bf16[128,4,1024]{2,1,0:T(4,128)(2,1)}), bf16[128,4,1024]{2,1,0:T(4,128)(2,1)S(1)}, u32[]{:S(2)}, u32[]{:S(2)}) async-start(bf16[128,4,1024]{2,1,0:T(4,128)(2,1)} %broadcast_select_fusion), calls=%async_computation.1 | async-start | bytes 2097152 | tf_op jit(solution)/shard_map/all_to_all | solution.py:57
  47.2 0.5 broadcast.156
  47.8 0.8 reduce.4
  48.7 28.9 %all-to-all-done.1 = bf16[128,4,1024]{2,1,0:T(4,128)(2,1)S(1)} async-done(((bf16[128,4,1024]{2,1,0:T(4,128)(2,1)}), bf16[128,4,1024]{2,1,0:T(4,128)(2,1)S(1)}, u32[]{:S(2)}, u32[]{:S(2)}) %all-to-all-start.1) | async-done | bytes 1048608 | tf_op jit(solution)/shard_map/all_to_all | solution.py:57
  77.6 1.1 reshape.130
  78.7 1.6 fusion.55
  80.3 26.3 %while.17 = (s32[]{:T(128)}, f32[1024,512]{1,0:T(8,128)}, f32[128,1024]{1,0:T(8,128)S(1)}, bf16[2,256,1024]{2,1,0:T(8,128)(2,1)}, bf16[2,256,1024]{2,1,0:T(8,128...) while((s32[]{:T(128)}, f32[1024,512]{1,0:T(8,128)}, ...), condition=%wide.region_4.5_spmd.clone, body=%wide.region_1.4_spmd.clone.sunk | while | flops 1055984640 | bytes 24351720 | solution.py:71
  80.5 2.5 fusion.107
  83.0 0.6 dynamic_slice.43
  83.6 0.6 iota_compare_fusion.6
  85.2 1.3 fusion.108
  87.9 0.6 fusion.112
  88.5 1.2 fusion.113
  89.7 3.1 select_add_fusion.2
  93.3 2.5 fusion.107
  95.8 0.6 dynamic_slice.43
  96.4 0.6 iota_compare_fusion.6
  98.0 1.3 fusion.108
  100.6 0.6 fusion.112
  101.3 1.2 fusion.113
  102.4 3.8 select_add_fusion.2
  106.6 1.0 copy.17
  107.7 274.3 %all-reduce.9.cloned.1.call-done = (f32[1024,512]{1,0:T(8,128)}, f32[128,1024]{0,1:T(8,128)}) async-done(((f32[1024,512]{1,0:T(8,128)}, f32[128,1024]{0,1:T(8,128)}), (f32[1024,512]{1,0:T(8,128)}, f32[128,1024]{0,1:T(8,128)})) %all-reduce.9.cloned.1.call-update) | async-done | bytes 2621456
  381.9 1.3 constant_dynamic-slice_fusion.1
  383.3 1.2 constant_dynamic-slice_fusion
  (52 shorter events, 5.6 us)
Async XLA Ops:
  7.2 21.9 %copy-start = (bf16[256,1024]{1,0:T(8,128)(2,1)S(1)}, bf16[256,1024]{1,0:T(8,128)(2,1)}, u32[]{:S(2)}) copy-start(bf16[256,1024]{1,0:T(8,128)(2,1)} %param.9) | copy-start | bytes 1572868
  8.7 29.9 %all-to-all-start = ((s32[128,1,4]{2,1,0:T(1,128)}), s32[128,1,4]{2,1,0:T(1,128)S(1)}, u32[]{:S(2)}, u32[]{:S(2)}) async-start(s32[128,1,4]{2,1,0:T(1,128)} %bitcast), calls=%async_computation | async-start | bytes 131072 | tf_op jit(solution)/shard_map/all_to_all | solution.py:58
  31.1 0.7 copy-start.2
  38.5 39.0 %all-to-all-start.1 = ((bf16[128,4,1024]{2,1,0:T(4,128)(2,1)}), bf16[128,4,1024]{2,1,0:T(4,128)(2,1)S(1)}, u32[]{:S(2)}, u32[]{:S(2)}) async-start(bf16[128,4,1024]{2,1,0:T(4,128)(2,1)} %broadcast_select_fusion), calls=%async_computation.1 | async-start | bytes 2097152 | tf_op jit(solution)/shard_map/all_to_all | solution.py:57
  47.1 33.2 %copy-start.1 = (bf16[2,256,1024]{2,1,0:T(8,128)(2,1)S(1)}, bf16[2,256,1024]{2,1,0:T(8,128)(2,1)}, u32[]{:S(2)}) copy-start(bf16[2,256,1024]{2,1,0:T(8,128)(2,1)} %param.12) | copy-start | bytes 3145732
  47.2 33.2 %copy-start.4 = (s32[2]{0:T(128)S(1)}, s32[2]{0:T(128)}, u32[]{:S(2)}) copy-start(s32[2]{0:T(128)} %param.13) | copy-start | bytes 28
  47.2 334.8 %all-reduce.9.cloned.1.call-start = ((), (), s32[]{:S(2)}) async-start(), calls=%async_computation.2 | async-start | bytes 5242880
  86.5 1.2 copy-start.3
  86.5 1.3 copy-start.5
  99.3 1.2 copy-start.3
  99.3 1.3 copy-start.5
Sparse Core Ops, SparseCore 0:
  107.8 274.1 all-reduce.8
where the time goes:
time: 393 us; the launch traced here: 391 us
  waiting for transfers between devices  308 us (78%)
  starting transfers between devices  27.1 us (7%)
  matrix products  20.6 us (5%)
  between operations  14.2 us (4%)
  local copies, waits for them, and re-layouts  12.1 us (3%)
  other arithmetic  7.57 us (2%)
    unnamed x2, waiting for transfers between devices  274 us
    all_to_all x1, waiting for transfers between devices, body(): lax.all_to_all(picked, 'own', split_axis=0, concat_axis=0, tiled=True)  28.9 us
    all_to_all x1, starting transfers between devices, body(): lax.all_to_all(send_user, 'own', split_axis=0, concat_axis=0, tiled=True)  18.4 us
    dot_general x6, matrix products, encode(): jnp.dot(normed, wi_f.astype(jnp.bfloat16), preferred_element_type=jnp.flo...  13.1 us
    all_to_all x1, starting transfers between devices, body(): lax.all_to_all(picked, 'own', split_axis=0, concat_axis=0, tiled=True)  8.6 us
  transfers between devices with their start and end apart: 3, of which 3 were waited for; matrix products, arithmetic and copies ran while one was open for 2% of the time, Pallas kernels for 0%

commit v1 on v0

v1 whole, which is shorter than its diff:
```python
import jax
import jax.numpy as jnp
from jax import lax
from jax.experimental import pallas as pl
from jax.experimental.pallas import tpu as pltpu
from jax.sharding import PartitionSpec as P

MESH = pl.DeviceIdType.MESH
F32, BF16, I32 = jnp.float32, jnp.bfloat16, jnp.int32
D, HD, L = 1024, 128, 256
RING = (4, 3, 5, 2, 6, 1, 7)
NT = (((1,), (1,)), ((), ()))
TN = (((0,), (0,)), ((), ()))


def mm(a, b, dims=(((1,), (0,)), ((), ()))):
    return lax.dot_general(a, b, dims, preferred_element_type=F32)


def kernel(
    len_s, cnt_v, slot_v, sg_h, hist_h, wi_h, wo_h,
    dx_h, gin_v, gout_v,
    sg, hist, wi, wo, dxb,
    tb, tr, ub, ua, gs1, gr1, gs2, gr2, row1, row2,
    pz, py, xz, xy,
    gate, att, wgt, dsw, pj, dsl, rs, dz, dzr, mvec,
    cb, cr, own, xb, xr, sm, smr, xs, xsr, zb, zr, yb, yr, zs2, zr2, ys2, yr2,
    load, send, recv,
):
    o_id = lax.axis_index("own")
    x = lax.axis_index("rep")
    y, z, c = o_id // 16, (o_id // 2) % 8, o_id % 2

    def at(dy=0, dz_=0, dc=0, dx=0):
        return (((lax.rem(y + dy, 8) * 8 + lax.rem(z + dz_, 8)) * 2 + lax.rem(c + dc, 2)), lax.rem(x + dx, 4))

    def put(src, dst, s, r, dev):
        return pltpu.make_async_remote_copy(
            src_ref=src, dst_ref=dst, send_sem=send.at[s], recv_sem=recv.at[r], device_id=dev, device_id_type=MESH
        )

    loads = [
        pltpu.make_async_copy(a, b, load.at[i])
        for i, (a, b) in enumerate(((sg_h, sg), (hist_h, hist), (wi_h, wi), (wo_h, wo)))
    ]
    for ld in loads:
        ld.start()

    barrier = pltpu.get_barrier_semaphore()
    peers = [at(dc=1)] + [at(dy=k) for k in RING] + [at(dz_=k) for k in RING] + [at(dx=k) for k in (2, 1, 3)]
    for dev in peers:
        pl.semaphore_signal(barrier, 1, device_id=dev, device_id_type=MESH)

    cnt = cnt_v[...].astype(F32)
    slots = slot_v[...].astype(F32).astype(BF16)
    ri = lax.broadcasted_iota(I32, (256, 1), 0)
    lane = lax.broadcasted_iota(I32, (256, 128), 1)
    samp = lax.broadcasted_iota(I32, (256, 256), 1).astype(F32)
    user = lax.rem(ri, 2).astype(F32)
    hi, mid, lo = ri // 128, lax.rem(ri // 16, 8), lax.rem(ri // 2, 8)

    def onehot(ry_, rz_):
        oi = (lax.rem(y + ry_, 8) * 8 + lax.rem(z + rz_, 8)) * 2 + lax.rem(c + 1 - hi + 2, 2)
        off = jnp.sum(jnp.where(lane < oi, cnt, 0.0), axis=1, keepdims=True)
        n = jnp.sum(jnp.where(lane == oi, cnt, 0.0), axis=1, keepdims=True)
        su = mm((lane == oi).astype(F32).astype(BF16), slots, NT)
        d = samp - off
        hit = jnp.zeros((256, 256), F32)
        for k in range(4):
            live = jnp.where((n > k) & (su[:, k : k + 1] == user), 1.0, 0.0)
            hit = hit + jnp.where(d == k, live, 0.0)
        return hit.astype(BF16)

    a1 = onehot(lo, mid)
    a2 = onehot(mid, lo)
    loads[0].wait()
    t1 = mm(a1, sg[:, 0:512])
    tb[0:128, :] = t1[0:128].astype(BF16)
    tb[256:384, :] = t1[128:256].astype(BF16)
    t2 = mm(a2, sg[:, 512:1024])
    tb[128:256, :] = t2[0:128].astype(BF16)
    tb[384:512, :] = t2[128:256].astype(BF16)

    pl.semaphore_wait(barrier, len(peers))
    core_g = put(tb.at[0:256], tr, 0, 0, at(dc=1))
    core_g.start()

    loads[1].wait()
    pr = lax.broadcasted_iota(I32, (256, 1), 0)
    fl = lax.broadcasted_iota(I32, (256, D), 1)

    def order(i, zfirst):
        r = pr + i * 256
        crel, xrel, m8, l8, j = r // 512, lax.rem(r // 128, 4), lax.rem(r // 16, 8), lax.rem(r // 2, 8), lax.rem(r, 2)
        ry_, rz_ = (l8, m8) if zfirst else (m8, l8)
        f = (lax.rem(y + ry_, 8) * 8 + lax.rem(z + rz_, 8)) * 2 + lax.rem(c + 1 - crel + 2, 2)
        f = f * 8 + lax.rem(x + xrel, 4) * 2 + j
        return (fl == f).astype(F32).astype(BF16)

    def permute(zfirst, pm, out):
        def step(i, carry):
            rows = pl.ds(pl.multiple_of(i * 256, 256), 256)
            pm[rows, :] = order(i, zfirst)
            for h in range(2):
                out[rows, h * L : (h + 1) * L] = mm(pm[rows, :], hist[h], NT).astype(BF16)
            return carry

        lax.fori_loop(0, 4, step, 0)

    permute(True, pz, xz)

    core_g.wait_recv()
    ua[...] = tb[256:512, :].astype(F32) + tr[...].astype(F32)
    ub[...] = ua[...].astype(BF16)
    for k in RING:
        a = slice(16 * k, 16 * k + 16)
        b = slice(128 + 16 * k, 128 + 16 * k + 16)
        put(ub.at[a], row1.at[a], 1, 1, at(dz_=k)).start()
        put(ub.at[b], row2.at[a], 2, 2, at(dy=k)).start()

    loads[2].wait()
    loads[3].wait()
    ti = lax.broadcasted_iota(I32, (L, 1), 0)
    tj = lax.broadcasted_iota(I32, (L, L), 1)

    def forward(h, carry):
        n = len_s[h]
        inv = 1.0 / jnp.full((1, 1), n, I32).astype(F32)
        xf = hist[h].astype(F32)
        r = lax.rsqrt(jnp.sum(xf * xf, axis=1, keepdims=True) * (1.0 / D) + 1e-05)
        rs[h] = jnp.broadcast_to(r, (L, HD))
        zz = mm((xf * r).astype(BF16), wi[...])
        sig = 1.0 / (1.0 + jnp.exp(-zz))
        p = zz * sig
        dsl[h] = sig + p * (1.0 - sig)
        gate[h] = p[:, 0:HD]
        pj[h] = p[:, HD:].astype(BF16)
        s = mm(pj[h, :, HD : 2 * HD], pj[h, :, 2 * HD :], NT) * HD**-0.5
        vis = (tj <= ti) & (tj < n)
        ss = 1.0 / (1.0 + jnp.exp(-s))
        sw = s * ss
        wgt[h] = (jnp.where(vis, sw, 0.0) * inv).astype(BF16)
        dsw[h] = jnp.where(vis, ss + sw * (1.0 - ss), 0.0) * (inv * HD**-0.5)
        at_ = mm(wgt[h], pj[h, :, 0:HD])
        att[h] = at_
        keep = jnp.where(ti < n, 1.0, 0.0) * inv
        mixed = (at_ * gate[h]).astype(BF16).astype(F32)
        mvec[h] = jnp.broadcast_to(jnp.sum(mixed * keep, axis=0, keepdims=True), (8, HD))
        return carry

    lax.fori_loop(0, 2, forward, 0)

    put(ub.at[16:128], row1.at[16:128], 1, 1, at(dz_=1)).wait_recv()
    put(ub.at[16:128], row2.at[16:128], 2, 2, at(dy=1)).wait_recv()
    s1, s2 = ua[0:16, :], ua[128:144, :]
    for k in range(1, 8):
        s1 = s1 + row1[16 * k : 16 * k + 16, :].astype(F32)
        s2 = s2 + row2[16 * k : 16 * k + 16, :].astype(F32)
    for k in range(8):
        gs1[k] = s1[2 * k : 2 * k + 2]
        gs2[k] = s2[2 * k : 2 * k + 2]
    for k in RING:
        put(gs1.at[k], gr1.at[k], 3, 3, at(dy=k)).start()
        put(gs2.at[k], gr2.at[k], 4, 4, at(dz_=k)).start()
    gr1[0] = s1[0:2]
    gr2[0] = s2[0:2]

    permute(False, py, xy)

    put(gs1.at[1:8], gr1.at[1:8], 3, 3, at(dy=1)).wait_recv()
    put(gs2.at[1:8], gr2.at[1:8], 4, 4, at(dz_=1)).wait_recv()
    g = jnp.concatenate([jnp.sum(gr1[...], axis=0), jnp.sum(gr2[...], axis=0)], axis=1)
    g8 = jnp.concatenate([g, jnp.zeros((6, D), F32)], axis=0)
    gb = g8.astype(BF16)
    v = mm(gb, wo[...], NT)

    for h in range(2):
        n = len_s[h]
        inv = 1.0 / jnp.full((1, 1), n, I32).astype(F32)
        keep = jnp.where(ti < n, 1.0, 0.0) * inv
        dm = keep * v[h : h + 1, :]
        datt = (dm * gate[h]).astype(BF16)
        dgate = dm * att[h]
        dval = mm(wgt[h], datt, TN)
        ds = (mm(datt, pj[h, :, 0:HD], NT) * dsw[h]).astype(BF16)
        dq = mm(ds, pj[h, :, 2 * HD :])
        dk = mm(ds, pj[h, :, HD : 2 * HD], TN)
        hr = slice(h * L, (h + 1) * L)
        for i, part in enumerate((dgate, dval, dq, dk)):
            cols = slice(i * HD, (i + 1) * HD)
            full = part * dsl[h, :, cols]
            dz[hr, cols] = full.astype(BF16)
            dzr[hr, cols] = (full * rs[h]).astype(BF16)

    cb[0:512, :] = mm(xz[0:512, :], dzr[:, 0:256]).astype(BF16)
    cz = put(cb.at[0:512], cr.at[0:512], 5, 5, at(dc=1))
    cz.start()
    cb[512:1024, :] = mm(xy[0:512, :], dzr[:, 256:512]).astype(BF16)
    cy = put(cb.at[512:1024], cr.at[512:1024], 6, 6, at(dc=1))
    cy.start()
    gp = mm(gb, pz[...], NT)
    m2 = jnp.concatenate([mvec[0, 0:1, :], mvec[1, 0:1, :]], axis=0)
    sm[0:2, :] = gp[0:2, 0:512]
    sm[2:4, 0:HD] = m2
    sm[2:4, HD:512] = jnp.zeros((2, 512 - HD), F32)
    sm[4:8, :] = jnp.zeros((4, 512), F32)
    cs = put(sm, smr, 7, 7, at(dc=1))
    cs.start()
    own[0:512, :] = mm(xz[512:1024, :], dzr[:, 0:256])
    own[512:1024, :] = mm(xy[512:1024, :], dzr[:, 256:512])
    for k in range(4):
        xs[k, 0:2, :] = gp[0:2, 512 + k * HD : 512 + (k + 1) * HD]
        xs[k, 4:6, :] = m2

    cz.wait_recv()
    cy.wait_recv()
    cs.wait_recv()
    for k in (2, 1, 3):
        a = slice(k * 128, (k + 1) * 128)
        b = slice(512 + k * 128, 512 + (k + 1) * 128)
        xb[k, 0:128, :] = (own[a, :] + cr[a, :].astype(F32)).astype(BF16)
        xb[k, 128:256, :] = (own[b, :] + cr[b, :].astype(F32)).astype(BF16)
        put(xb.at[k], xr.at[k], 8, 8, at(dx=k)).start()
    for k in range(4):
        xs[k, 2:4, :] = smr[0:2, k * HD : (k + 1) * HD]
        xs[k, 6:8, :] = smr[2:4, 0:HD]
    for k in (2, 1, 3):
        put(xs.at[k], xsr.at[k], 9, 9, at(dx=k)).start()
    xsr[0] = xs[0]

    def back(h, carry):
        n = len_s[h]
        inv = 1.0 / jnp.full((1, 1), n, I32).astype(F32)
        keep = jnp.where(ti < n, 1.0, 0.0) * inv
        dn = mm(dz[pl.ds(pl.multiple_of(h * L, L), L), :], wi[...], NT)
        r = rs[h, :, 0:1]
        xn = hist[h].astype(F32) * r
        mean = jnp.sum(dn * xn, axis=1, keepdims=True) * (1.0 / D)
        gh = jnp.where(h == 0, g[0:1, :], g[1:2, :])
        dxb[h] = (r * (dn - xn * mean) + keep * gh).astype(BF16)
        return carry

    lax.fori_loop(0, 2, back, 0)
    out = pltpu.make_async_copy(dxb, dx_h, load.at[4])
    out.start()

    put(xb.at[1:4], xr.at[1:4], 8, 8, at(dx=1)).wait_recv()
    put(xs.at[1:4], xsr.at[1:4], 9, 9, at(dx=1)).wait_recv()
    gx = jnp.concatenate([xsr[k, 0:4, :] for k in range(4)], axis=0)
    mx = jnp.concatenate([xsr[k, 4:8, :] for k in range(4)], axis=0)
    sz = own[0:128, :] + cr[0:128, :].astype(F32)
    sy = own[512:640, :] + cr[512:640, :].astype(F32)
    for k in range(1, 4):
        sz = sz + xr[k, 0:128, :].astype(F32)
        sy = sy + xr[k, 128:256, :].astype(F32)
    so = mm(gx.astype(BF16), mx.astype(BF16), TN)
    zb[:, 0:256] = sz.astype(BF16)
    zb[:, 256:384] = so.astype(BF16)
    yb[...] = sy.astype(BF16)
    for k in RING:
        a = slice(16 * k, 16 * k + 16)
        put(zb.at[a], zr.at[a], 10, 10, at(dz_=k)).start()
        put(yb.at[a], yr.at[a], 11, 11, at(dy=k)).start()
    z0 = jnp.concatenate([sz[0:16], so[0:16]], axis=1)
    y0 = sy[0:16]
    put(zb.at[16:128], zr.at[16:128], 10, 10, at(dz_=1)).wait_recv()
    put(yb.at[16:128], yr.at[16:128], 11, 11, at(dy=1)).wait_recv()
    for k in range(1, 8):
        z0 = z0 + zr[16 * k : 16 * k + 16, :].astype(F32)
        y0 = y0 + yr[16 * k : 16 * k + 16, :].astype(F32)
    for k in range(8):
        zs2[k] = z0[2 * k : 2 * k + 2]
        ys2[k] = y0[2 * k : 2 * k + 2]
    for k in RING:
        put(zs2.at[k], zr2.at[k], 12, 12, at(dy=k)).start()
        put(ys2.at[k], yr2.at[k], 13, 13, at(dz_=k)).start()
    zr2[0] = z0[0:2]
    yr2[0] = y0[0:2]

    core_g.wait_send()
    put(ub.at[16:128], row1.at[16:128], 1, 1, at(dz_=1)).wait_send()
    put(ub.at[16:128], row2.at[16:128], 2, 2, at(dy=1)).wait_send()
    put(gs1.at[1:8], gr1.at[1:8], 3, 3, at(dy=1)).wait_send()
    put(gs2.at[1:8], gr2.at[1:8], 4, 4, at(dz_=1)).wait_send()
    cz.wait_send()
    cy.wait_send()
    cs.wait_send()
    put(xb.at[1:4], xr.at[1:4], 8, 8, at(dx=1)).wait_send()
    put(xs.at[1:4], xsr.at[1:4], 9, 9, at(dx=1)).wait_send()
    put(zb.at[16:128], zr.at[16:128], 10, 10, at(dz_=1)).wait_send()
    put(yb.at[16:128], yr.at[16:128], 11, 11, at(dy=1)).wait_send()
    out.wait()

    put(zs2.at[1:8], zr2.at[1:8], 12, 12, at(dy=1)).wait()
    put(ys2.at[1:8], yr2.at[1:8], 13, 13, at(dz_=1)).wait()
    fz = jnp.sum(zr2[...], axis=0)
    fy = jnp.sum(yr2[...], axis=0)
    gin_v[:, 0:256] = fz[:, 0:256]
    gin_v[:, 256:512] = fy
    gout_v[...] = fz[:, 256:384]


def finish(dx_h, gin_h, gout_h, dx_o, gin_o, gout_o, sem):
    copies = [
        pltpu.make_async_copy(a, b, sem.at[i])
        for i, (a, b) in enumerate(((dx_h, dx_o), (gin_h, gin_o), (gout_h, gout_o)))
    ]
    for copy in copies:
        copy.start()
    for copy in copies:
        copy.wait()


def body(sample_grads, send_count, send_user, histories, hist_len, w_in, w_out):
    vm = pl.BlockSpec(memory_space=pltpu.VMEM)
    hbm = pl.BlockSpec(memory_space=pl.ANY)
    sd = jax.ShapeDtypeStruct
    V = pltpu.VMEM
    dx, gin, gout = pl.pallas_call(
        kernel,
        out_shape=(sd((2, L, D), BF16), sd((2, 512), F32), sd((2, HD), F32)),
        in_specs=[pl.BlockSpec(memory_space=pltpu.SMEM), vm, vm, hbm, hbm, hbm, hbm],
        out_specs=(hbm, vm, vm),
        scratch_shapes=[
            V((256, D), BF16), V((2, L, D), BF16), V((D, 512), BF16), V((HD, D), BF16), V((2, L, D), BF16),
            V((512, 512), BF16), V((256, 512), BF16), V((256, 512), BF16), V((256, 512), F32),
            V((8, 2, 512), F32), V((8, 2, 512), F32), V((8, 2, 512), F32), V((8, 2, 512), F32),
            V((128, 512), BF16), V((128, 512), BF16),
            V((D, D), BF16), V((D, D), BF16), V((D, 512), BF16), V((D, 512), BF16),
            V((2, L, HD), F32), V((2, L, HD), F32), V((2, L, L), BF16), V((2, L, L), F32),
            V((2, L, 3 * HD), BF16), V((2, L, 512), F32), V((2, L, HD), F32),
            V((512, 512), BF16), V((512, 512), BF16), V((2, 8, HD), F32),
            V((1024, 256), BF16), V((1024, 256), BF16), V((1024, 256), F32),
            V((4, 256, 256), BF16), V((4, 256, 256), BF16),
            V((8, 512), F32), V((8, 512), F32), V((4, 8, HD), F32), V((4, 8, HD), F32),
            V((128, 384), BF16), V((128, 384), BF16), V((128, 256), BF16), V((128, 256), BF16),
            V((8, 2, 384), F32), V((8, 2, 384), F32), V((8, 2, 256), F32), V((8, 2, 256), F32),
            pltpu.SemaphoreType.DMA((5,)), pltpu.SemaphoreType.DMA((14,)), pltpu.SemaphoreType.DMA((14,)),
        ],
        compiler_params=pltpu.CompilerParams(
            collective_id=0, has_side_effects=True, vmem_limit_bytes=62 * 1024 * 1024
        ),
        name="encoder_backward",
    )(hist_len, send_count, send_user.T, sample_grads, histories, w_in, w_out)
    dx, gin, gout = pl.pallas_call(
        finish,
        out_shape=(sd((2, L, D), BF16), sd((2, 512), F32), sd((2, HD), F32)),
        in_specs=[hbm, hbm, hbm],
        out_specs=(hbm, hbm, hbm),
        scratch_shapes=[pltpu.SemaphoreType.DMA((3,))],
        compiler_params=pltpu.CompilerParams(vmem_limit_bytes=62 * 1024 * 1024),
        name="finish",
    )(dx, gin, gout)
    return dx, gin, gout.T


def solution(mesh):
    both = ("own", "rep")
    return jax.shard_map(
        body,
        mesh=mesh,
        in_specs=(P(both, None), P(both, None), P(both, None), P(both, None, None), P(both), P(), P()),
        out_specs=(P(both, None, None), P(both, None), P(None, both)),
        check_vma=False,
    )
```

time: 393 us -> 84.7 us (0.22)
  waiting for transfers between devices: 308 us -> 0 us
  Pallas kernels: 0 us -> 83.8 us
  starting transfers between devices: 27.1 us -> 0 us
  matrix products: 20.6 us -> 0 us
  between operations: 14.2 us -> 0.64 us
  local copies, waits for them, and re-layouts: 12.1 us -> 0 us
  other arithmetic: 7.57 us -> 0 us
    unnamed x2 -> x0, waiting for transfers between devices: 274 us -> none
    pallas_call x0 -> x2, Pallas kernels: none -> 83.8 us  [the longest x1 50.8 us: body(): pl.pallas_call(kernel, out_shape=(sd((2, L, D), BF16), sd((2, 512), F32),...]
    all_to_all x2 -> x0, waiting for transfers between devices: 34 us -> none  [the longest x1 28.9 us: body(): lax.all_to_all(picked, 'own', split_axis=0, concat_axis=0, tiled=True)]
    all_to_all x2 -> x0, starting transfers between devices: 27 us -> none  [the longest x1 18.4 us: body(): lax.all_to_all(send_user, 'own', split_axis=0, concat_axis=0, tiled=True)]
    dot_general x23 -> x0, matrix products: 20.6 us -> none  [the longest x6 13.1 us: encode(): jnp.dot(normed, wi_f.astype(jnp.bfloat16), preferred_element_type=jnp.flo...]
    unnamed x11 -> x0, local copies, waits for them, and re-layouts: 4.26 us -> none
  transfers between devices with their start and end apart: 3 -> 0, of which waited for: 3 -> 0; matrix products, arithmetic and copies ran while one was open for 2% -> 0% of each run, Pallas kernels for 0% -> 0%
where the time goes in v1:
time: 84.7 us; the launch traced here: 84.5 us
  Pallas kernels  83.8 us (99%)
    pallas_call x1, Pallas kernels, body(): pl.pallas_call(kernel, out_shape=(sd((2, L, D), BF16), sd((2, 512), F32),...  50.8 us
    pallas_call x1, Pallas kernels, body(): pl.pallas_call(finish, out_shape=(sd((2, L, D), BF16), sd((2, 512), F32),...  33 us

profile of v1, /device:TPU:1, one launch (start us, length us, event | category | flops | bytes accessed | tf_op | source)
XLA Modules:
  0.0 84.5 jit_solution(9432357388989445007)
XLA Ops:
  0.6 50.8 %encoder_backward.1 = (bf16[2,256,1024]{2,1,0:T(8,128)(2,1)}, f32[2,512]{1,0:T(2,128)}, f32[2,128]{1,0:T(2,128)}) custom-call(s32[2]{0:T(128)} %len_s.1, s32[1,128]{1,0:T(1,128)} %cnt_v.1, s32[4,128]{1,0:T(4,128)} %bitcast.2, bf16[256,1024]{1,0:T(8,128)(2,1)} %sg_h.1, bf16[2,256,1024]{2,1,0:T(8,128)(2,1)} %hist_h.1, bf16[1024,512]{1,0:T(8,128)(2,1)} %wi_h.1, ...), custom_call_target="tpu_custom_call" | custom-call | tf_op jit(solution)/shard_map/encoder_backward/pallas_call | solution.py:319
  51.4 33.0 %finish.1 = (bf16[2,256,1024]{2,1,0:T(8,128)(2,1)}, f32[2,512]{1,0:T(2,128)}, f32[2,128]{1,0:T(2,128)}) custom-call(bf16[2,256,1024]{2,1,0:T(8,128)(2,1)} %get-tuple-element.9.dx_h, f32[2,512]{1,0:T(2,128)} %get-tuple-element.10.gin_h, f32[2,128]{1,0:T(2,128)} %get-tuple-element.11.gout_h), custom_call_target="tpu_custom_call" | custom-call | tf_op jit(solution)/shard_map/finish/pallas_call | solution.py:345

commit v2 on v0

v2 whole, which is shorter than its diff:
```python
import jax
import jax.numpy as jnp
from jax import lax
from jax.experimental import pallas as pl
from jax.experimental.pallas import tpu as pltpu
from jax.sharding import PartitionSpec as P

MESH = pl.DeviceIdType.MESH
F32, BF16, I32 = jnp.float32, jnp.bfloat16, jnp.int32
D, HD, L = 1024, 128, 256
VMEM = 61 * 1024 * 1024
VMEM = 61 * 1024 * 1024
VMEM = 61 * 1024 * 1024
VMEM = 61 * 1024 * 1024
RING = (4, 3, 5, 2, 6, 1, 7)
NT = (((1,), (1,)), ((), ()))
TN = (((0,), (0,)), ((), ()))


def mm(a, b, dims=(((1,), (0,)), ((), ()))):
    return lax.dot_general(a, b, dims, preferred_element_type=F32)


def kernel(
    len_s, cnt_h, slot_h, sg_h, hist_h, wi_h, wo_h,
    dx_o, gin_o, gout_o,
    cnt_v, slot_v, sg, hist, wi, wo,
    tv, vr, vb, vzr, vys, vyr,
    tb, tr, ua, ub, gzr, gys, gyr,
    pz, xz,
    kgate, pre, preg, wgt, dsw, pj, dsl, rs, dz, dzr, mvec, cpre,
    cb, cr, own, xb, xr, sm, smr, xs, xsr, zb, zr, yb, yr, zs2, zr2, ys2, yr2,
    load, send, recv,
):
    o_id = lax.axis_index("own")
    x = lax.axis_index("rep")
    y, z, c = o_id // 16, (o_id // 2) % 8, o_id % 2

    def at(dy=0, dz_=0, dc=0, dx=0):
        return (((lax.rem(y + dy, 8) * 8 + lax.rem(z + dz_, 8)) * 2 + lax.rem(c + dc, 2)), lax.rem(x + dx, 4))

    def put(src, dst, i, dev):
        return pltpu.make_async_remote_copy(
            src_ref=src, dst_ref=dst, send_sem=send.at[i], recv_sem=recv.at[i], device_id=dev, device_id_type=MESH
        )

    def many(src, dst, i, axis, rows=None):
        for k in (2, 1, 3) if axis == "dx" else RING:
            a = k if rows is None else slice(rows * k, rows * k + rows)
            put(src.at[a], dst.at[a], i, at(**{axis: k})).start()

    def whole(src, dst, i, axis, rows=None):
        n = 4 if axis == "dx" else 8
        a = slice(1, n) if rows is None else slice(rows, rows * n)
        return put(src.at[a], dst.at[a], i, at(**{axis: 1}))

    loads = [
        pltpu.make_async_copy(a, b, load.at[i])
        for i, (a, b) in enumerate(
            ((cnt_h, cnt_v), (slot_h, slot_v), (sg_h, sg), (wo_h, wo), (hist_h, hist), (wi_h, wi))
        )
    ]
    for ld in loads:
        ld.start()

    barrier = pltpu.get_barrier_semaphore()
    peers = [at(dc=1)] + [at(dy=k) for k in RING] + [at(dz_=k) for k in RING] + [at(dx=k) for k in (2, 1, 3)]
    for dev in peers:
        pl.semaphore_signal(barrier, 1, device_id=dev, device_id_type=MESH)

    ri = lax.broadcasted_iota(I32, (256, 1), 0)
    lane = lax.broadcasted_iota(I32, (256, 128), 1)
    samp = lax.broadcasted_iota(I32, (256, 256), 1).astype(F32)
    user = lax.rem(ri, 2).astype(F32)
    oi = (lax.rem(y + lax.rem(ri // 2, 8), 8) * 8 + lax.rem(z + lax.rem(ri // 16, 8), 8)) * 2
    oi = oi + lax.rem(c + 1 - ri // 128 + 2, 2)
    loads[0].wait()
    loads[1].wait()
    cnt = cnt_v[...].astype(F32)
    slots = slot_v[...].astype(F32).astype(BF16)
    off = jnp.sum(jnp.where(lane < oi, cnt, 0.0), axis=1, keepdims=True)
    num = jnp.sum(jnp.where(lane == oi, cnt, 0.0), axis=1, keepdims=True)
    su = mm((lane == oi).astype(F32).astype(BF16), slots, NT)
    d = samp - off
    hit = jnp.zeros((256, 256), F32)
    for k in range(4):
        live = jnp.where((num > k) & (su[:, k : k + 1] == user), 1.0, 0.0)
        hit = hit + jnp.where(d == k, live, 0.0)
    hit = hit.astype(BF16)
    loads[2].wait()
    loads[3].wait()
    tv[...] = mm(hit, mm(sg[...], wo[...], NT).astype(BF16))

    pl.semaphore_wait(barrier, len(peers))
    v_core = put(tv.at[0:128], vr, 0, at(dc=1))
    v_core.start()
    tb[...] = mm(hit[0:128], sg[...]).astype(BF16)
    g_core = put(tb, tr, 1, at(dc=1))
    g_core.start()
    ua[...] = mm(hit[128:256], sg[...])
    v_core.wait_recv()
    vb[...] = tv[128:256, :] + vr[...]
    many(vb, vzr, 2, "dz_", 16)
    g_core.wait_recv()
    ua[...] = ua[...] + tr[...].astype(F32)
    ub[...] = ua[...].astype(BF16)
    many(ub, gzr, 3, "dz_", 16)

    loads[4].wait()
    loads[5].wait()
    ti = lax.broadcasted_iota(I32, (L, 1), 0)
    tj = lax.broadcasted_iota(I32, (L, L), 1)

    def shares(h):
        n = len_s[h]
        inv = 1.0 / jnp.full((1, 1), n, I32).astype(F32)
        return n, inv, jnp.where(ti < n, 1.0, 0.0) * inv

    def forward(h, carry):
        n, inv, keep = shares(h)
        xf = hist[h].astype(F32)
        r = lax.rsqrt(jnp.sum(xf * xf, axis=1, keepdims=True) * (1.0 / D) + 1e-05)
        rs[h] = jnp.broadcast_to(r, (L, HD))
        zz = mm((xf * r).astype(BF16), wi[...])
        sig = 1.0 / (1.0 + jnp.exp(-zz))
        p = zz * sig
        ds = sig + p * (1.0 - sig)
        dsl[h] = ds[:, 2 * HD :]
        pj[h] = p[:, HD:].astype(BF16)
        s = mm(pj[h, :, HD : 2 * HD], pj[h, :, 2 * HD :], NT) * HD**-0.5
        vis = (tj <= ti) & (tj < n)
        ss = 1.0 / (1.0 + jnp.exp(-s))
        sw = s * ss
        wgt[h] = (jnp.where(vis, sw, 0.0) * inv).astype(BF16)
        dsw[h] = jnp.where(vis, ss + sw * (1.0 - ss), 0.0) * (inv * HD**-0.5)
        att = mm(wgt[h], pj[h, :, 0:HD])
        mixed = (att * p[:, 0:HD]).astype(BF16).astype(F32)
        mvec[h] = jnp.broadcast_to(jnp.sum(mixed * keep, axis=0, keepdims=True), (8, HD))
        kg = keep * p[:, 0:HD]
        kgate[h] = kg
        pg = keep * att * ds[:, 0:HD]
        pv = mm(wgt[h], kg.astype(BF16), TN) * ds[:, HD : 2 * HD]
        pre[h, :, 0:HD] = pg
        pre[h, :, HD:] = pv
        preg[h, :, 0:HD] = (pg * r).astype(BF16)
        preg[h, :, HD:] = (pv * r).astype(BF16)
        return carry

    lax.fori_loop(0, 2, forward, 0)

    pr = lax.broadcasted_iota(I32, (256, 1), 0)
    fl = lax.broadcasted_iota(I32, (256, D), 1)

    def permute(i, carry):
        r = pr + i * 256
        crel, xrel, j, m8, l8 = r // 512, lax.rem(r // 128, 4), lax.rem(r // 64, 2), lax.rem(r // 8, 8), lax.rem(r, 8)
        ry_, rz_ = jnp.where(j == 0, l8, m8), jnp.where(j == 0, m8, l8)
        f = (lax.rem(y + ry_, 8) * 8 + lax.rem(z + rz_, 8)) * 2 + lax.rem(c + 1 - crel + 2, 2)
        f = f * 8 + lax.rem(x + xrel, 4) * 2 + j
        rows = pl.ds(pl.multiple_of(i * 256, 256), 256)
        pm = (fl == f).astype(F32).astype(BF16)
        pz[rows, :] = pm
        for h in range(2):
            xz[rows, h * L : (h + 1) * L] = mm(pm, hist[h], NT).astype(BF16)
            cpre[h, rows, :] = mm(xz[rows, h * L : (h + 1) * L], preg[h])
        return carry

    lax.fori_loop(0, 2, permute, 0)
    whole(vb, vzr, 2, "dz_", 16).wait_recv()
    s1 = vb[0:16, :]
    for k in range(1, 8):
        s1 = s1 + vzr[16 * k : 16 * k + 16, :]
    for k in range(8):
        vys[k] = s1[2 * k : 2 * k + 2]
    many(vys, vyr, 4, "dy")
    vyr[0] = s1[0:2]

    lax.fori_loop(2, 4, permute, 0)
    whole(ub, gzr, 3, "dz_", 16).wait_recv()
    s1 = ua[0:16, :]
    for k in range(1, 8):
        s1 = s1 + gzr[16 * k : 16 * k + 16, :].astype(F32)
    for k in range(8):
        gys[k] = s1[2 * k : 2 * k + 2]
    many(gys, gyr, 5, "dy")
    gyr[0] = s1[0:2]

    whole(vys, vyr, 4, "dy").wait_recv()
    v = jnp.sum(vyr[...], axis=0)
    va = jnp.concatenate([v[0:1], v[0:1]], axis=1)
    vc = jnp.concatenate([v[1:2], v[1:2]], axis=1)
    cb[0:512, :] = (cpre[0, 0:512, :] * va + cpre[1, 0:512, :] * vc).astype(BF16)
    c1 = put(cb.at[0:512], cr.at[0:512], 6, at(dc=1))
    c1.start()
    for h in range(2):
        datt = (kgate[h] * v[h : h + 1, :]).astype(BF16)
        ds = (mm(datt, pj[h, :, 0:HD], NT) * dsw[h]).astype(BF16)
        dq = mm(ds, pj[h, :, 2 * HD :])
        dk = mm(ds, pj[h, :, HD : 2 * HD], TN)
        hr = slice(h * L, (h + 1) * L)
        for i, part in enumerate((dq, dk)):
            full = part * dsl[h, :, i * HD : (i + 1) * HD]
            dz[hr, (i + 2) * HD : (i + 3) * HD] = full.astype(BF16)
            dzr[hr, i * HD : (i + 1) * HD] = (full * rs[h]).astype(BF16)
    cb[512:1024, :] = mm(xz[0:512, :], dzr[...]).astype(BF16)
    c2 = put(cb.at[512:1024], cr.at[512:1024], 7, at(dc=1))
    c2.start()
    own[0:512, :] = cpre[0, 512:1024, :] * va + cpre[1, 512:1024, :] * vc
    c1.wait_recv()

    def xsums(p, i):
        for k in (2, 1, 3):
            a = slice(p * 512 + k * 128, p * 512 + (k + 1) * 128)
            xb[p, k] = (own[a, :] + cr[a, :].astype(F32)).astype(BF16)
            put(xb.at[p, k], xr.at[p, k], i, at(dx=k)).start()

    xsums(0, 8)
    own[512:1024, :] = mm(xz[512:1024, :], dzr[...])
    c2.wait_recv()
    xsums(1, 9)

    whole(gys, gyr, 5, "dy").wait_recv()
    g = jnp.sum(gyr[...], axis=0)
    gp = mm(jnp.concatenate([g, jnp.zeros((6, D), F32)], axis=0).astype(BF16), pz[...], NT)
    m2 = jnp.concatenate([mvec[0, 0:1, :], mvec[1, 0:1, :]], axis=0)
    sm[0:2, :] = gp[0:2, 0:512]
    sm[2:4, 0:HD] = m2
    sm[2:4, HD:512] = jnp.zeros((2, 512 - HD), F32)
    sm[4:8, :] = jnp.zeros((4, 512), F32)
    cs = put(sm, smr, 10, at(dc=1))
    cs.start()
    for k in range(4):
        xs[k, 0:2, :] = gp[0:2, 512 + k * HD : 512 + (k + 1) * HD]
        xs[k, 4:6, :] = m2

    def back(h, carry):
        n, inv, keep = shares(h)
        hr = pl.ds(pl.multiple_of(h * L, L), L)
        vh = jnp.where(h == 0, va, vc)
        dz[hr, 0 : 2 * HD] = (pre[h] * vh).astype(BF16)
        dn = mm(dz[hr, :], wi[...], NT)
        r = rs[h, :, 0:1]
        xn = hist[h].astype(F32) * r
        mean = jnp.sum(dn * xn, axis=1, keepdims=True) * (1.0 / D)
        gh = jnp.where(h == 0, g[0:1, :], g[1:2, :])
        dx_o[h] = (r * (dn - xn * mean) + keep * gh).astype(BF16)
        return carry

    lax.fori_loop(0, 1, back, 0)
    cs.wait_recv()
    for k in range(4):
        xs[k, 2:4, :] = smr[0:2, k * HD : (k + 1) * HD]
        xs[k, 6:8, :] = smr[2:4, 0:HD]
    many(xs, xsr, 11, "dx")
    xsr[0] = xs[0]
    lax.fori_loop(1, 2, back, 0)

    def xtotal(p, i):
        put(xb.at[p, 1:4], xr.at[p, 1:4], i, at(dx=1)).wait_recv()
        t = own[p * 512 : p * 512 + 128, :] + cr[p * 512 : p * 512 + 128, :].astype(F32)
        for k in range(1, 4):
            t = t + xr[p, k].astype(F32)
        return t

    t0 = xtotal(0, 8)
    whole(xs, xsr, 11, "dx").wait_recv()
    gx = jnp.concatenate([xsr[k, 0:4, :] for k in range(4)], axis=0)
    mx = jnp.concatenate([xsr[k, 4:8, :] for k in range(4)], axis=0)
    so = mm(gx.astype(BF16), mx.astype(BF16), TN)
    t1 = xtotal(1, 9)

    def packed(a):
        p = jnp.concatenate([t0[a], so[a]], axis=1).reshape(8, 8, 384)
        q = jnp.concatenate([t1[a], jnp.zeros((64, HD), F32)], axis=1).reshape(8, 8, 384)
        return jnp.concatenate([p, q], axis=1).reshape(128, 384)

    z0 = packed(slice(0, 64))
    zb[...] = z0.astype(BF16)
    many(zb, zr, 12, "dz_", 16)
    y0 = packed(slice(64, 128))
    yb[...] = y0.astype(BF16)
    many(yb, yr, 13, "dy", 16)

    def total(first, src, dst, i, axis, out, got, j, other):
        whole(src, dst, i, axis, 16).wait_recv()
        t = first[0:16]
        for k in range(1, 8):
            t = t + dst[16 * k : 16 * k + 16, :].astype(F32)
        t = jnp.concatenate([t[0:8, 0:256], t[8:16, 0:256], t[0:8, 256:384]], axis=1)
        for k in range(8):
            out[k] = jnp.broadcast_to(t[k : k + 1], (2, 640))
        many(out, got, j, other)
        got[0] = jnp.broadcast_to(t[0:1], (2, 640))

    total(z0, zb, zr, 12, "dz_", zs2, zr2, 14, "dy")
    total(y0, yb, yr, 13, "dy", ys2, yr2, 15, "dz_")

    for cp in (v_core, g_core, c1, c2, cs):
        cp.wait_send()
    whole(vb, vzr, 2, "dz_", 16).wait_send()
    whole(ub, gzr, 3, "dz_", 16).wait_send()
    whole(vys, vyr, 4, "dy").wait_send()
    whole(gys, gyr, 5, "dy").wait_send()
    put(xb.at[0, 1:4], xr.at[0, 1:4], 8, at(dx=1)).wait_send()
    put(xb.at[1, 1:4], xr.at[1, 1:4], 9, at(dx=1)).wait_send()
    whole(xs, xsr, 11, "dx").wait_send()
    whole(zb, zr, 12, "dz_", 16).wait_send()
    whole(yb, yr, 13, "dy", 16).wait_send()

    whole(zs2, zr2, 14, "dy").wait()
    fz = jnp.sum(zr2[...], axis=0)
    whole(ys2, yr2, 15, "dz_").wait()
    fy = jnp.sum(yr2[...], axis=0)
    gin_o[0:1, :] = fz[0:1, 0:512]
    gin_o[1:2, :] = fy[0:1, 0:512]
    gout_o[0:1, :] = fz[0:1, 512:640]
    gout_o[1:2, :] = fy[0:1, 512:640]


def finish(dx_v, gin_v, gout_v, dx_o, gin_o, gout_o, sem):
    copies = [
        pltpu.make_async_copy(a, b, sem.at[i])
        for i, (a, b) in enumerate(((dx_v, dx_o), (gin_v, gin_o), (gout_v, gout_o)))
    ]
    for copy in copies:
        copy.start()
    for copy in copies:
        copy.wait()


def body(sample_grads, send_count, send_user, histories, hist_len, w_in, w_out):
    vm = pl.BlockSpec(memory_space=pltpu.VMEM)
    hbm = pl.BlockSpec(memory_space=pl.ANY)
    V = pltpu.VMEM
    sd = jax.ShapeDtypeStruct
    dx, gin, gout = pl.pallas_call(
        kernel,
        out_shape=(V((2, L, D), BF16), V((2, 512), F32), V((2, HD), F32)),
        in_specs=[pl.BlockSpec(memory_space=pltpu.SMEM), hbm, hbm, hbm, hbm, hbm, hbm],
        out_specs=(vm, vm, vm),
        scratch_shapes=[
            V((1, 128), I32), V((4, 128), I32), V((256, D), BF16), V((2, L, D), BF16), V((D, 512), BF16), V((HD, D), BF16),
            V((256, HD), F32), V((128, HD), F32), V((128, HD), F32), V((128, HD), F32), V((8, 2, HD), F32), V((8, 2, HD), F32),
            V((128, D), BF16), V((128, D), BF16), V((128, D), F32), V((128, D), BF16), V((128, D), BF16),
            V((8, 2, D), F32), V((8, 2, D), F32),
            V((D, D), BF16), V((D, 512), BF16),
            V((2, L, HD), F32), V((2, L, 256), F32), V((2, L, 256), BF16), V((2, L, L), BF16), V((2, L, L), F32),
            V((2, L, 3 * HD), BF16), V((2, L, 256), F32), V((2, L, HD), F32),
            V((512, 512), BF16), V((512, 256), BF16), V((2, 8, HD), F32), V((2, D, 256), F32),
            V((1024, 256), BF16), V((1024, 256), BF16), V((1024, 256), F32),
            V((2, 4, 128, 256), BF16), V((2, 4, 128, 256), BF16),
            V((8, 512), F32), V((8, 512), F32), V((4, 8, HD), F32), V((4, 8, HD), F32),
            V((128, 384), BF16), V((128, 384), BF16), V((128, 384), BF16), V((128, 384), BF16),
            V((8, 2, 640), F32), V((8, 2, 640), F32), V((8, 2, 640), F32), V((8, 2, 640), F32),
            pltpu.SemaphoreType.DMA((6,)), pltpu.SemaphoreType.DMA((16,)), pltpu.SemaphoreType.DMA((16,)),
        ],
        compiler_params=pltpu.CompilerParams(
            collective_id=0, has_side_effects=True, vmem_limit_bytes=VMEM
        ),
        name="encoder_backward",
    )(hist_len, send_count, send_user.T, sample_grads, histories, w_in, w_out)
    dx, gin, gout = pl.pallas_call(
        finish,
        out_shape=(sd((2, L, D), BF16), sd((2, 512), F32), sd((2, HD), F32)),
        in_specs=[vm, vm, vm],
        out_specs=(hbm, hbm, hbm),
        scratch_shapes=[pltpu.SemaphoreType.DMA((3,))],
        compiler_params=pltpu.CompilerParams(vmem_limit_bytes=8 * 1024 * 1024),
        name="finish",
    )(dx, gin, gout)
    return dx, gin, gout.T


def solution(mesh):
    both = ("own", "rep")
    return jax.shard_map(
        body,
        mesh=mesh,
        in_specs=(P(both, None), P(both, None), P(both, None), P(both, None, None), P(both), P(), P()),
        out_specs=(P(both, None, None), P(both, None), P(None, both)),
        check_vma=False,
    )
```

time: 393 us -> 48 us (0.12)
  waiting for transfers between devices: 308 us -> 0 us
  Pallas kernels: 0 us -> 46.7 us
  starting transfers between devices: 27.1 us -> 0 us
  matrix products: 20.6 us -> 0 us
  between operations: 14.2 us -> 0.64 us
  local copies, waits for them, and re-layouts: 12.1 us -> 0 us
  other arithmetic: 7.57 us -> 0 us
    unnamed x2 -> x0, waiting for transfers between devices: 274 us -> none
    pallas_call x0 -> x2, Pallas kernels: none -> 46.7 us  [the longest x1 45.7 us: body(): pl.pallas_call(kernel, out_shape=(V((2, L, D), BF16), V((2, 512), F32), V...]
    all_to_all x2 -> x0, waiting for transfers between devices: 34 us -> none  [the longest x1 28.9 us: body(): lax.all_to_all(picked, 'own', split_axis=0, concat_axis=0, tiled=True)]
    all_to_all x2 -> x0, starting transfers between devices: 27 us -> none  [the longest x1 18.4 us: body(): lax.all_to_all(send_user, 'own', split_axis=0, concat_axis=0, tiled=True)]
    dot_general x23 -> x0, matrix products: 20.6 us -> none  [the longest x6 13.1 us: encode(): jnp.dot(normed, wi_f.astype(jnp.bfloat16), preferred_element_type=jnp.flo...]
    unnamed x11 -> x0, local copies, waits for them, and re-layouts: 4.26 us -> none
  transfers between devices with their start and end apart: 3 -> 0, of which waited for: 3 -> 0; matrix products, arithmetic and copies ran while one was open for 2% -> 0% of each run, Pallas kernels for 0% -> 0%
where the time goes in v2:
time: 48 us; the launch traced here: 47.4 us
  Pallas kernels  46.7 us (97%)
  between operations  0.64 us (1%)
    pallas_call x1, Pallas kernels, body(): pl.pallas_call(kernel, out_shape=(V((2, L, D), BF16), V((2, 512), F32), V...  45.7 us
    pallas_call x1, Pallas kernels, body(): pl.pallas_call(finish, out_shape=(sd((2, L, D), BF16), sd((2, 512), F32),...  1 us

profile of v2, /device:TPU:1, one launch (start us, length us, event | category | flops | bytes accessed | tf_op | source)
XLA Modules:
  0.0 47.4 jit_solution(4305770943467350871)
XLA Ops:
  0.6 45.7 %encoder_backward.1 = (bf16[2,256,1024]{2,1,0:T(8,128)(2,1)S(1)}, f32[2,512]{1,0:T(2,128)S(1)}, f32[2,128]{1,0:T(2,128)S(1)}) custom-call(s32[2]{0:T(128)} %len_s.1, s32[1,128]{1,0:T(1,128)} %cnt_h.1, s32[4,128]{1,0:T(4,128)} %bitcast.2, bf16[256,1024]{1,0:T(8,128)(2,1)} %sg_h.1, bf16[2,256,1024]{2,1,0:T(8,128)(2,1)} %hist_h.1, bf16[1024,512]{1,0:T(8,128)(2,1)} %wi_h.1, ...), custom_call_target="tpu_custom_call" | custom-call | tf_op jit(solution)/shard_map/encoder_backward/pallas_call | solution.py:336
  46.4 1.0 %finish.1 = (bf16[2,256,1024]{2,1,0:T(8,128)(2,1)}, f32[2,512]{1,0:T(2,128)}, f32[2,128]{1,0:T(2,128)}) custom-call(bf16[2,256,1024]{2,1,0:T(8,128)(2,1)S(1)} %get-tuple-element.9.dx_v, f32[2,512]{1,0:T(2,128)S(1)} %get-tuple-element.10.gin_v, f32[2,128]{1,0:T(2,128)S(1)} %get-tuple-element.11.gout_v), custom_call_target="tpu_custom_call" | custom-call | tf_op jit(solution)/shard_map/finish/pallas_call | solution.py:362

commit v3 on v2

--- a/solution.py
+++ b/solution.py
@@ -9,9 +9,6 @@
 F32, BF16, I32 = jnp.float32, jnp.bfloat16, jnp.int32
 D, HD, L = 1024, 128, 256
 VMEM = 61 * 1024 * 1024
-VMEM = 61 * 1024 * 1024
-VMEM = 61 * 1024 * 1024
-VMEM = 61 * 1024 * 1024
 RING = (4, 3, 5, 2, 6, 1, 7)
 NT = (((1,), (1,)), ((), ()))
 TN = (((0,), (0,)), ((), ()))
@@ -25,19 +22,20 @@
     len_s, cnt_h, slot_h, sg_h, hist_h, wi_h, wo_h,
     dx_o, gin_o, gout_o,
     cnt_v, slot_v, sg, hist, wi, wo,
-    tv, vr, vb, vzr, vys, vyr,
+    tv, tvb, vzr, vys, vyr, vfin,
     tb, tr, ua, ub, gzr, gys, gyr,
     pz, xz,
     kgate, pre, preg, wgt, dsw, pj, dsl, rs, dz, dzr, mvec, cpre,
-    cb, cr, own, xb, xr, sm, smr, xs, xsr, zb, zr, yb, yr, zs2, zr2, ys2, yr2,
+    cb, cr, own, xb, xr, gm, gmr, fbt, fb, fr,
     load, send, recv,
 ):
     o_id = lax.axis_index("own")
     x = lax.axis_index("rep")
     y, z, c = o_id // 16, (o_id // 2) % 8, o_id % 2
 
-    def at(dy=0, dz_=0, dc=0, dx=0):
-        return (((lax.rem(y + dy, 8) * 8 + lax.rem(z + dz_, 8)) * 2 + lax.rem(c + dc, 2)), lax.rem(x + dx, 4))
+    def at(dy=0, dz_=0, dc=0, dx=0, core=None):
+        k = lax.rem(c + dc, 2) if core is None else core
+        return (lax.rem(y + dy, 8) * 8 + lax.rem(z + dz_, 8)) * 2 + k, lax.rem(x + dx, 4)
 
     def put(src, dst, i, dev):
         return pltpu.make_async_remote_copy(
@@ -68,39 +66,55 @@
     for dev in peers:
         pl.semaphore_signal(barrier, 1, device_id=dev, device_id_type=MESH)
 
+    @pl.when(c == 1)
+    def _():
+        for k in RING:
+            pl.semaphore_signal(barrier, 1, device_id=at(dz_=k, core=0), device_id_type=MESH)
+
     ri = lax.broadcasted_iota(I32, (256, 1), 0)
     lane = lax.broadcasted_iota(I32, (256, 128), 1)
     samp = lax.broadcasted_iota(I32, (256, 256), 1).astype(F32)
     user = lax.rem(ri, 2).astype(F32)
-    oi = (lax.rem(y + lax.rem(ri // 2, 8), 8) * 8 + lax.rem(z + lax.rem(ri // 16, 8), 8)) * 2
-    oi = oi + lax.rem(c + 1 - ri // 128 + 2, 2)
     loads[0].wait()
     loads[1].wait()
     cnt = cnt_v[...].astype(F32)
     slots = slot_v[...].astype(F32).astype(BF16)
-    off = jnp.sum(jnp.where(lane < oi, cnt, 0.0), axis=1, keepdims=True)
-    num = jnp.sum(jnp.where(lane == oi, cnt, 0.0), axis=1, keepdims=True)
-    su = mm((lane == oi).astype(F32).astype(BF16), slots, NT)
-    d = samp - off
-    hit = jnp.zeros((256, 256), F32)
-    for k in range(4):
-        live = jnp.where((num > k) & (su[:, k : k + 1] == user), 1.0, 0.0)
-        hit = hit + jnp.where(d == k, live, 0.0)
-    hit = hit.astype(BF16)
+
+    def onehot(ry_, rz_, core):
+        oi = (lax.rem(y + ry_, 8) * 8 + lax.rem(z + rz_, 8)) * 2 + core
+        off = jnp.sum(jnp.where(lane < oi, cnt, 0.0), axis=1, keepdims=True)
+        num = jnp.sum(jnp.where(lane == oi, cnt, 0.0), axis=1, keepdims=True)
+        su = mm((lane == oi).astype(F32).astype(BF16), slots, NT)
+        d = samp - off
+        hit = jnp.zeros((256, 256), F32)
+        for k in range(4):
+            live = jnp.where((num > k) & (su[:, k : k + 1] == user), 1.0, 0.0)
+            hit = hit + jnp.where(d == k, live, 0.0)
+        return hit.astype(BF16)
+
+    hit = onehot(lax.rem(ri // 4, 8), ri // 32, lax.rem(ri // 2, 2))
     loads[2].wait()
     loads[3].wait()
     tv[...] = mm(hit, mm(sg[...], wo[...], NT).astype(BF16))
-
-    pl.semaphore_wait(barrier, len(peers))
-    v_core = put(tv.at[0:128], vr, 0, at(dc=1))
-    v_core.start()
+    tvb[...] = tv[...].astype(BF16)
+
+    def vput(k):
+        slot = pl.ds(pl.multiple_of((k + 7 * c) * 32, 32), 32)
+        return put(tvb.at[32 * k : 32 * k + 32], vzr.at[slot], 0, at(dz_=k, core=1))
+
+    pl.semaphore_wait(barrier, len(peers) + 7 * (1 - c))
+    for k in RING:
+        vput(k).start()
+
+    @pl.when(c == 0)
+    def _():
+        put(tvb.at[0:32], vzr.at[0:32], 0, at(dc=1)).start()
+
+    hit = onehot(lax.rem(ri // 2, 8), lax.rem(ri // 16, 8), lax.rem(c + 1 - ri // 128 + 2, 2))
     tb[...] = mm(hit[0:128], sg[...]).astype(BF16)
     g_core = put(tb, tr, 1, at(dc=1))
     g_core.start()
     ua[...] = mm(hit[128:256], sg[...])
-    v_core.wait_recv()
-    vb[...] = tv[128:256, :] + vr[...]
-    many(vb, vzr, 2, "dz_", 16)
     g_core.wait_recv()
     ua[...] = ua[...] + tr[...].astype(F32)
     ub[...] = ua[...].astype(BF16)
@@ -153,8 +167,7 @@
 
     def permute(i, carry):
         r = pr + i * 256
-        crel, xrel, j, m8, l8 = r // 512, lax.rem(r // 128, 4), lax.rem(r // 64, 2), lax.rem(r // 8, 8), lax.rem(r, 8)
-        ry_, rz_ = jnp.where(j == 0, l8, m8), jnp.where(j == 0, m8, l8)
+        crel, xrel, ry_, rz_, j = r // 512, lax.rem(r // 128, 4), lax.rem(r // 16, 8), lax.rem(r // 2, 8), lax.rem(r, 2)
         f = (lax.rem(y + ry_, 8) * 8 + lax.rem(z + rz_, 8)) * 2 + lax.rem(c + 1 - crel + 2, 2)
         f = f * 8 + lax.rem(x + xrel, 4) * 2 + j
         rows = pl.ds(pl.multiple_of(i * 256, 256), 256)
@@ -166,16 +179,37 @@
         return carry
 
     lax.fori_loop(0, 2, permute, 0)
-    whole(vb, vzr, 2, "dz_", 16).wait_recv()
-    s1 = vb[0:16, :]
-    for k in range(1, 8):
-        s1 = s1 + vzr[16 * k : 16 * k + 16, :]
-    for k in range(8):
-        vys[k] = s1[2 * k : 2 * k + 2]
-    many(vys, vyr, 4, "dy")
-    vyr[0] = s1[0:2]
+
+    @pl.when(c == 1)
+    def _():
+        put(vzr.at[0:480], vzr.at[0:480], 0, at(dc=1)).wait_recv()
+        s = tv[0:32, :]
+        for k in range(15):
+            s = s + vzr[32 * k : 32 * k + 32, :].astype(F32)
+        for k in range(8):
+            vys[k] = s[4 * k : 4 * k + 4]
+        many(vys, vyr, 2, "dy")
+        vyr[0] = s[0:4]
 
     lax.fori_loop(2, 4, permute, 0)
+    v_core = put(vfin, vfin, 4, at(dc=1))
+
+    @pl.when(c == 1)
+    def _():
+        whole(vys, vyr, 2, "dy").wait_recv()
+        vfin[...] = jnp.sum(vyr[...], axis=0)
+        v_core.start()
+
+    @pl.when(c == 0)
+    def _():
+        v_core.wait_recv()
+
+    v = jnp.where(c == 0, vfin[0:2, :], vfin[2:4, :])
+    va = jnp.concatenate([v[0:1], v[0:1]], axis=1)
+    vc = jnp.concatenate([v[1:2], v[1:2]], axis=1)
+    cb[0:512, :] = (cpre[0, 0:512, :] * va + cpre[1, 0:512, :] * vc).astype(BF16)
+    c1 = put(cb.at[0:512], cr.at[0:512], 6, at(dc=1))
+    c1.start()
     whole(ub, gzr, 3, "dz_", 16).wait_recv()
     s1 = ua[0:16, :]
     for k in range(1, 8):
@@ -184,14 +218,6 @@
         gys[k] = s1[2 * k : 2 * k + 2]
     many(gys, gyr, 5, "dy")
     gyr[0] = s1[0:2]
-
-    whole(vys, vyr, 4, "dy").wait_recv()
-    v = jnp.sum(vyr[...], axis=0)
-    va = jnp.concatenate([v[0:1], v[0:1]], axis=1)
-    vc = jnp.concatenate([v[1:2], v[1:2]], axis=1)
-    cb[0:512, :] = (cpre[0, 0:512, :] * va + cpre[1, 0:512, :] * vc).astype(BF16)
-    c1 = put(cb.at[0:512], cr.at[0:512], 6, at(dc=1))
-    c1.start()
     for h in range(2):
         datt = (kgate[h] * v[h : h + 1, :]).astype(BF16)
         ds = (mm(datt, pj[h, :, 0:HD], NT) * dsw[h]).astype(BF16)
@@ -223,15 +249,14 @@
     g = jnp.sum(gyr[...], axis=0)
     gp = mm(jnp.concatenate([g, jnp.zeros((6, D), F32)], axis=0).astype(BF16), pz[...], NT)
     m2 = jnp.concatenate([mvec[0, 0:1, :], mvec[1, 0:1, :]], axis=0)
-    sm[0:2, :] = gp[0:2, 0:512]
-    sm[2:4, 0:HD] = m2
-    sm[2:4, HD:512] = jnp.zeros((2, 512 - HD), F32)
-    sm[4:8, :] = jnp.zeros((4, 512), F32)
-    cs = put(sm, smr, 10, at(dc=1))
-    cs.start()
-    for k in range(4):
-        xs[k, 0:2, :] = gp[0:2, 512 + k * HD : 512 + (k + 1) * HD]
-        xs[k, 4:6, :] = m2
+    for dc in range(2):
+        for dx in range(4):
+            q = (1 - dc) * 4 + dx
+            gm[dc * 4 + dx, 0:2, :] = gp[0:2, q * HD : (q + 1) * HD]
+            gm[dc * 4 + dx, 2:4, :] = m2
+    for k in (6, 2, 5, 7, 1, 3, 4):
+        put(gm.at[k], gmr.at[k], 10, at(dc=k // 4, dx=k % 4)).start()
+    gmr[0] = gm[0]
 
     def back(h, carry):
         n, inv, keep = shares(h)
@@ -246,14 +271,7 @@
         dx_o[h] = (r * (dn - xn * mean) + keep * gh).astype(BF16)
         return carry
 
-    lax.fori_loop(0, 1, back, 0)
-    cs.wait_recv()
-    for k in range(4):
-        xs[k, 2:4, :] = smr[0:2, k * HD : (k + 1) * HD]
-        xs[k, 6:8, :] = smr[2:4, 0:HD]
-    many(xs, xsr, 11, "dx")
-    xsr[0] = xs[0]
-    lax.fori_loop(1, 2, back, 0)
+    lax.fori_loop(0, 2, back, 0)
 
     def xtotal(p, i):
         put(xb.at[p, 1:4], xr.at[p, 1:4], i, at(dx=1)).wait_recv()
@@ -263,65 +281,48 @@
         return t
 
     t0 = xtotal(0, 8)
-    whole(xs, xsr, 11, "dx").wait_recv()
-    gx = jnp.concatenate([xsr[k, 0:4, :] for k in range(4)], axis=0)
-    mx = jnp.concatenate([xsr[k, 4:8, :] for k in range(4)], axis=0)
+    t1 = xtotal(1, 9)
+    put(gm.at[1:8], gmr.at[1:8], 10, at(dc=1)).wait_recv()
+    gx = jnp.concatenate([gmr[k, 0:2, :] for k in range(8)], axis=0)
+    mx = jnp.concatenate([gmr[k, 2:4, :] for k in range(8)], axis=0)
     so = mm(gx.astype(BF16), mx.astype(BF16), TN)
-    t1 = xtotal(1, 9)
-
-    def packed(a):
-        p = jnp.concatenate([t0[a], so[a]], axis=1).reshape(8, 8, 384)
-        q = jnp.concatenate([t1[a], jnp.zeros((64, HD), F32)], axis=1).reshape(8, 8, 384)
-        return jnp.concatenate([p, q], axis=1).reshape(128, 384)
-
-    z0 = packed(slice(0, 64))
-    zb[...] = z0.astype(BF16)
-    many(zb, zr, 12, "dz_", 16)
-    y0 = packed(slice(64, 128))
-    yb[...] = y0.astype(BF16)
-    many(yb, yr, 13, "dy", 16)
-
-    def total(first, src, dst, i, axis, out, got, j, other):
-        whole(src, dst, i, axis, 16).wait_recv()
-        t = first[0:16]
-        for k in range(1, 8):
-            t = t + dst[16 * k : 16 * k + 16, :].astype(F32)
-        t = jnp.concatenate([t[0:8, 0:256], t[8:16, 0:256], t[0:8, 256:384]], axis=1)
-        for k in range(8):
-            out[k] = jnp.broadcast_to(t[k : k + 1], (2, 640))
-        many(out, got, j, other)
-        got[0] = jnp.broadcast_to(t[0:1], (2, 640))
-
-    total(z0, zb, zr, 12, "dz_", zs2, zr2, 14, "dy")
-    total(y0, yb, yr, 13, "dy", ys2, yr2, 15, "dz_")
-
-    for cp in (v_core, g_core, c1, c2, cs):
+    t = jnp.concatenate([t0, t1, so], axis=1)
+    fbt[...] = t.astype(BF16)
+    for a in RING + (0,):
+        for b in RING + (0,):
+            k = a * 8 + b
+            if k:
+                fb[k] = fbt[2 * k : 2 * k + 2, :]
+                put(fb.at[k], fr.at[k], 11, at(dy=a, dz_=b)).start()
+
+    @pl.when(c == 0)
+    def _():
+        put(tvb, tvb, 0, at(dc=1)).wait_send()
+
+    @pl.when(c == 1)
+    def _():
+        put(tvb.at[32:256], tvb.at[32:256], 0, at(dc=1)).wait_send()
+        whole(vys, vyr, 2, "dy").wait_send()
+        v_core.wait_send()
+
+    for cp in (g_core, c1, c2):
         cp.wait_send()
-    whole(vb, vzr, 2, "dz_", 16).wait_send()
     whole(ub, gzr, 3, "dz_", 16).wait_send()
-    whole(vys, vyr, 4, "dy").wait_send()
     whole(gys, gyr, 5, "dy").wait_send()
     put(xb.at[0, 1:4], xr.at[0, 1:4], 8, at(dx=1)).wait_send()
     put(xb.at[1, 1:4], xr.at[1, 1:4], 9, at(dx=1)).wait_send()
-    whole(xs, xsr, 11, "dx").wait_send()
-    whole(zb, zr, 12, "dz_", 16).wait_send()
-    whole(yb, yr, 13, "dy", 16).wait_send()
-
-    whole(zs2, zr2, 14, "dy").wait()
-    fz = jnp.sum(zr2[...], axis=0)
-    whole(ys2, yr2, 15, "dz_").wait()
-    fy = jnp.sum(yr2[...], axis=0)
-    gin_o[0:1, :] = fz[0:1, 0:512]
-    gin_o[1:2, :] = fy[0:1, 0:512]
-    gout_o[0:1, :] = fz[0:1, 512:640]
-    gout_o[1:2, :] = fy[0:1, 512:640]
+    put(gm.at[1:8], gmr.at[1:8], 10, at(dc=1)).wait_send()
+
+    put(fb.at[1:64], fr.at[1:64], 11, at(dy=1)).wait()
+    f = t[0:2, :] + jnp.sum(fr[1:64].astype(F32), axis=0)
+    gin_o[...] = f[:, 0:512]
+    gout_o[...] = f[:, 512:640]
 
 
 def finish(dx_v, gin_v, gout_v, dx_o, gin_o, gout_o, sem):
-    copies = [
-        pltpu.make_async_copy(a, b, sem.at[i])
-        for i, (a, b) in enumerate(((dx_v, dx_o), (gin_v, gin_o), (gout_v, gout_o)))
-    ]
+    pairs = [(dx_v.at[h, r : r + 128], dx_o.at[h, r : r + 128]) for h in range(2) for r in (0, 128)]
+    pairs += [(gin_v, gin_o), (gout_v, gout_o)]
+    copies = [pltpu.make_async_copy(a, b, sem.at[i]) for i, (a, b) in enumerate(pairs)]
     for copy in copies:
         copy.start()
     for copy in copies:
@@ -340,7 +341,7 @@
         out_specs=(vm, vm, vm),
         scratch_shapes=[
             V((1, 128), I32), V((4, 128), I32), V((256, D), BF16), V((2, L, D), BF16), V((D, 512), BF16), V((HD, D), BF16),
-            V((256, HD), F32), V((128, HD), F32), V((128, HD), F32), V((128, HD), F32), V((8, 2, HD), F32), V((8, 2, HD), F32),
+            V((256, HD), F32), V((256, HD), BF16), V((480, HD), BF16), V((8, 4, HD), F32), V((8, 4, HD), F32), V((4, HD), F32),
             V((128, D), BF16), V((128, D), BF16), V((128, D), F32), V((128, D), BF16), V((128, D), BF16),
             V((8, 2, D), F32), V((8, 2, D), F32),
             V((D, D), BF16), V((D, 512), BF16),
@@ -349,10 +350,8 @@
             V((512, 512), BF16), V((512, 256), BF16), V((2, 8, HD), F32), V((2, D, 256), F32),
             V((1024, 256), BF16), V((1024, 256), BF16), V((1024, 256), F32),
             V((2, 4, 128, 256), BF16), V((2, 4, 128, 256), BF16),
-            V((8, 512), F32), V((8, 512), F32), V((4, 8, HD), F32), V((4, 8, HD), F32),
-            V((128, 384), BF16), V((128, 384), BF16), V((128, 384), BF16), V((128, 384), BF16),
-            V((8, 2, 640), F32), V((8, 2, 640), F32), V((8, 2, 640), F32), V((8, 2, 640), F32),
-            pltpu.SemaphoreType.DMA((6,)), pltpu.SemaphoreType.DMA((16,)), pltpu.SemaphoreType.DMA((16,)),
+            V((8, 4, HD), F32), V((8, 4, HD), F32), V((128, 640), BF16), V((64, 2, 640), BF16), V((64, 2, 640), BF16),
+            pltpu.SemaphoreType.DMA((6,)), pltpu.SemaphoreType.DMA((12,)), pltpu.SemaphoreType.DMA((12,)),
         ],
         compiler_params=pltpu.CompilerParams(
             collective_id=0, has_side_effects=True, vmem_limit_bytes=VMEM
@@ -364,7 +363,7 @@
         out_shape=(sd((2, L, D), BF16), sd((2, 512), F32), sd((2, HD), F32)),
         in_specs=[vm, vm, vm],
         out_specs=(hbm, hbm, hbm),
-        scratch_shapes=[pltpu.SemaphoreType.DMA((3,))],
+        scratch_shapes=[pltpu.SemaphoreType.DMA((6,))],
         compiler_params=pltpu.CompilerParams(vmem_limit_bytes=8 * 1024 * 1024),
         name="finish",
     )(dx, gin, gout)

time: 48 us -> 46.8 us (0.975)
  Pallas kernels: 46.7 us -> 46 us
    pallas_call x1, Pallas kernels: 45.7 us -> 45 us  [body(): pl.pallas_call(kernel, out_shape=(V((2, L, D), BF16), V((2, 512), F32), V...]
where the time goes in v3:
time: 46.8 us; the launch traced here: 46.6 us
  Pallas kernels  46 us (98%)
  between operations  0.64 us (1%)
    pallas_call x1, Pallas kernels, body(): pl.pallas_call(kernel, out_shape=(V((2, L, D), BF16), V((2, 512), F32), V...  45 us
    pallas_call x1, Pallas kernels, body(): pl.pallas_call(finish, out_shape=(sd((2, L, D), BF16), sd((2, 512), F32),...  1.02 us

profile of v3, /device:TPU:1, one launch (start us, length us, event | category | flops | bytes accessed | tf_op | source)
XLA Modules:
  0.0 46.6 jit_solution(1429704372560245246)
XLA Ops:
  0.6 45.0 %encoder_backward.1 = (bf16[2,256,1024]{2,1,0:T(8,128)(2,1)S(1)}, f32[2,512]{1,0:T(2,128)S(1)}, f32[2,128]{1,0:T(2,128)S(1)}) custom-call(s32[2]{0:T(128)} %len_s.1, s32[1,128]{1,0:T(1,128)} %cnt_h.1, s32[4,128]{1,0:T(4,128)} %bitcast.2, bf16[256,1024]{1,0:T(8,128)(2,1)} %sg_h.1, bf16[2,256,1024]{2,1,0:T(8,128)(2,1)} %hist_h.1, bf16[1024,512]{1,0:T(8,128)(2,1)} %wi_h.1, ...), custom_call_target="tpu_custom_call" | custom-call | tf_op jit(solution)/shard_map/encoder_backward/pallas_call | solution.py:337
  45.6 1.0 %finish.1 = (bf16[2,256,1024]{2,1,0:T(8,128)(2,1)}, f32[2,512]{1,0:T(2,128)}, f32[2,128]{1,0:T(2,128)}) custom-call(bf16[2,256,1024]{2,1,0:T(8,128)(2,1)S(1)} %get-tuple-element.9.dx_v, f32[2,512]{1,0:T(2,128)S(1)} %get-tuple-element.10.gin_v, f32[2,128]{1,0:T(2,128)S(1)} %get-tuple-element.11.gout_v), custom_call_target="tpu_custom_call" | custom-call | tf_op jit(solution)/shard_map/finish/pallas_call | solution.py:361

commit v4 on v3

--- a/solution.py
+++ b/solution.py
@@ -24,9 +24,9 @@
     cnt_v, slot_v, sg, hist, wi, wo,
     tv, tvb, vzr, vys, vyr, vfin,
     tb, tr, ua, ub, gzr, gys, gyr,
-    pz, xz,
+    pz, xz, xq,
     kgate, pre, preg, wgt, dsw, pj, dsl, rs, dz, dzr, mvec, cpre,
-    cb, cr, own, xb, xr, gm, gmr, fbt, fb, fr,
+    cb, cr, own, kc, kcr, kown, xb, xr, kb, kr, gm, gmr, fbt, fb, fr, kf, kfr,
     load, send, recv,
 ):
     o_id = lax.axis_index("own")
@@ -52,14 +52,15 @@
         a = slice(1, n) if rows is None else slice(rows, rows * n)
         return put(src.at[a], dst.at[a], i, at(**{axis: 1}))
 
-    loads = [
-        pltpu.make_async_copy(a, b, load.at[i])
-        for i, (a, b) in enumerate(
-            ((cnt_h, cnt_v), (slot_h, slot_v), (sg_h, sg), (wo_h, wo), (hist_h, hist), (wi_h, wi))
-        )
-    ]
-    for ld in loads:
-        ld.start()
+    def fetch(i, src, dst):
+        cp = pltpu.make_async_copy(src, dst, load.at[i])
+        cp.start()
+        return cp
+
+    small = [fetch(0, cnt_h, cnt_v), fetch(1, slot_h, slot_v)]
+    for k in range(0, 256, 64):
+        pltpu.make_async_copy(sg_h.at[k : k + 64], sg.at[k : k + 64], load.at[2]).start()
+    small += [pltpu.make_async_copy(sg_h, sg, load.at[2]), fetch(3, wo_h, wo)]
 
     barrier = pltpu.get_barrier_semaphore()
     peers = [at(dc=1)] + [at(dy=k) for k in RING] + [at(dz_=k) for k in RING] + [at(dx=k) for k in (2, 1, 3)]
@@ -71,12 +72,14 @@
         for k in RING:
             pl.semaphore_signal(barrier, 1, device_id=at(dz_=k, core=0), device_id_type=MESH)
 
+    large = [fetch(4, hist_h, hist), fetch(5, wi_h, wi)]
+
     ri = lax.broadcasted_iota(I32, (256, 1), 0)
     lane = lax.broadcasted_iota(I32, (256, 128), 1)
     samp = lax.broadcasted_iota(I32, (256, 256), 1).astype(F32)
     user = lax.rem(ri, 2).astype(F32)
-    loads[0].wait()
-    loads[1].wait()
+    for cp in small:
+        cp.wait()
     cnt = cnt_v[...].astype(F32)
     slots = slot_v[...].astype(F32).astype(BF16)
 
@@ -93,8 +96,6 @@
         return hit.astype(BF16)
 
     hit = onehot(lax.rem(ri // 4, 8), ri // 32, lax.rem(ri // 2, 2))
-    loads[2].wait()
-    loads[3].wait()
     tv[...] = mm(hit, mm(sg[...], wo[...], NT).astype(BF16))
     tvb[...] = tv[...].astype(BF16)
 
@@ -111,17 +112,19 @@
         put(tvb.at[0:32], vzr.at[0:32], 0, at(dc=1)).start()
 
     hit = onehot(lax.rem(ri // 2, 8), lax.rem(ri // 16, 8), lax.rem(c + 1 - ri // 128 + 2, 2))
-    tb[...] = mm(hit[0:128], sg[...]).astype(BF16)
+    sr = lax.broadcasted_iota(I32, (128, 1), 0)
+    sl = lax.broadcasted_iota(I32, (128, 128), 1)
+    swap = (sl == lax.rem(sr // 2, 8) * 16 + sr // 16 * 2 + lax.rem(sr, 2)).astype(F32).astype(BF16)
+    other = jnp.concatenate([mm(swap, hit[0:128]), mm(swap, hit[128:256])], axis=0).astype(BF16)
+    tb[0:128, :] = mm(hit[0:128], sg[:, 0:512]).astype(BF16)
+    tb[128:256, :] = mm(other[0:128], sg[:, 512:]).astype(BF16)
     g_core = put(tb, tr, 1, at(dc=1))
     g_core.start()
-    ua[...] = mm(hit[128:256], sg[...])
-    g_core.wait_recv()
-    ua[...] = ua[...] + tr[...].astype(F32)
-    ub[...] = ua[...].astype(BF16)
-    many(ub, gzr, 3, "dz_", 16)
-
-    loads[4].wait()
-    loads[5].wait()
+    ua[0:128, :] = mm(hit[128:256], sg[:, 0:512])
+    ua[128:256, :] = mm(other[128:256], sg[:, 512:])
+
+    for cp in large:
+        cp.wait()
     ti = lax.broadcasted_iota(I32, (L, 1), 0)
     tj = lax.broadcasted_iota(I32, (L, L), 1)
 
@@ -160,25 +163,14 @@
         preg[h, :, HD:] = (pv * r).astype(BF16)
         return carry
 
-    lax.fori_loop(0, 2, forward, 0)
-
-    pr = lax.broadcasted_iota(I32, (256, 1), 0)
-    fl = lax.broadcasted_iota(I32, (256, D), 1)
-
-    def permute(i, carry):
-        r = pr + i * 256
-        crel, xrel, ry_, rz_, j = r // 512, lax.rem(r // 128, 4), lax.rem(r // 16, 8), lax.rem(r // 2, 8), lax.rem(r, 2)
-        f = (lax.rem(y + ry_, 8) * 8 + lax.rem(z + rz_, 8)) * 2 + lax.rem(c + 1 - crel + 2, 2)
-        f = f * 8 + lax.rem(x + xrel, 4) * 2 + j
-        rows = pl.ds(pl.multiple_of(i * 256, 256), 256)
-        pm = (fl == f).astype(F32).astype(BF16)
-        pz[rows, :] = pm
-        for h in range(2):
-            xz[rows, h * L : (h + 1) * L] = mm(pm, hist[h], NT).astype(BF16)
-            cpre[h, rows, :] = mm(xz[rows, h * L : (h + 1) * L], preg[h])
-        return carry
-
-    lax.fori_loop(0, 2, permute, 0)
+    lax.fori_loop(0, 1, forward, 0)
+    g_core.wait_recv()
+    ua[...] = ua[...] + tr[...].astype(F32)
+    ub[...] = ua[...].astype(BF16)
+    many(ub, gzr, 3, "dz_", 16)
+    many(ub.at[128:256], gzr.at[128:256], 15, "dy", 16)
+    lax.fori_loop(1, 2, forward, 0)
+
 
     @pl.when(c == 1)
     def _():
@@ -191,7 +183,39 @@
         many(vys, vyr, 2, "dy")
         vyr[0] = s[0:4]
 
-    lax.fori_loop(2, 4, permute, 0)
+    pr = lax.broadcasted_iota(I32, (512, 1), 0)
+    fl = lax.broadcasted_iota(I32, (512, D), 1)
+
+    def permute(i, carry):
+        r = pr + i * 512
+        crel, xrel, ry_, rz_, j = r // 512, lax.rem(r // 128, 4), lax.rem(r // 16, 8), lax.rem(r // 2, 8), lax.rem(r, 2)
+        f = (lax.rem(y + ry_, 8) * 8 + lax.rem(z + rz_, 8)) * 2 + lax.rem(c + 1 - crel + 2, 2)
+        f = f * 8 + lax.rem(x + xrel, 4) * 2 + j
+        rows = pl.ds(pl.multiple_of(i * 512, 512), 512)
+        pm = (fl == f).astype(F32).astype(BF16)
+        pz[rows, :] = pm
+        xz[rows, :] = mm(pm, hist[...].reshape(2 * L, D), NT).astype(BF16)
+        for h in range(2):
+            cpre[h, rows, :] = mm(xz[rows, h * L : (h + 1) * L], preg[h])
+        return carry
+
+    lax.fori_loop(0, 2, permute, 0)
+    for k in range(0, D, 128):
+        xq[k : k + 128, :] = mm(swap, xz[k : k + 128, :]).astype(BF16)
+
+    whole(ub, gzr, 3, "dz_", 16).wait_recv()
+    whole(ub.at[128:256], gzr.at[128:256], 15, "dy", 16).wait_recv()
+    mine = []
+    for p, i, axis in ((0, 5, "dy"), (1, 16, "dz_")):
+        s1 = ua[128 * p : 128 * p + 16, :]
+        for k in range(1, 8):
+            s1 = s1 + gzr[128 * p + 16 * k : 128 * p + 16 * k + 16, :].astype(F32)
+        mine.append(s1[0:2])
+        s1 = s1.astype(BF16)
+        for k in range(1, 8):
+            gys[p, k] = s1[2 * k : 2 * k + 2]
+        many(gys.at[p], gyr.at[p], i, axis)
+
     v_core = put(vfin, vfin, 4, at(dc=1))
 
     @pl.when(c == 1)
@@ -207,17 +231,6 @@
     v = jnp.where(c == 0, vfin[0:2, :], vfin[2:4, :])
     va = jnp.concatenate([v[0:1], v[0:1]], axis=1)
     vc = jnp.concatenate([v[1:2], v[1:2]], axis=1)
-    cb[0:512, :] = (cpre[0, 0:512, :] * va + cpre[1, 0:512, :] * vc).astype(BF16)
-    c1 = put(cb.at[0:512], cr.at[0:512], 6, at(dc=1))
-    c1.start()
-    whole(ub, gzr, 3, "dz_", 16).wait_recv()
-    s1 = ua[0:16, :]
-    for k in range(1, 8):
-        s1 = s1 + gzr[16 * k : 16 * k + 16, :].astype(F32)
-    for k in range(8):
-        gys[k] = s1[2 * k : 2 * k + 2]
-    many(gys, gyr, 5, "dy")
-    gyr[0] = s1[0:2]
     for h in range(2):
         datt = (kgate[h] * v[h : h + 1, :]).astype(BF16)
         ds = (mm(datt, pj[h, :, 0:HD], NT) * dsw[h]).astype(BF16)
@@ -228,25 +241,35 @@
             full = part * dsl[h, :, i * HD : (i + 1) * HD]
             dz[hr, (i + 2) * HD : (i + 3) * HD] = full.astype(BF16)
             dzr[hr, i * HD : (i + 1) * HD] = (full * rs[h]).astype(BF16)
-    cb[512:1024, :] = mm(xz[0:512, :], dzr[...]).astype(BF16)
-    c2 = put(cb.at[512:1024], cr.at[512:1024], 7, at(dc=1))
+
+    def regroup(r):
+        return jnp.concatenate([r[a * 128 + b * 16 : a * 128 + b * 16 + 16] for b in range(8) for a in range(4)], axis=0)
+
+    kc[0:512, :] = regroup(mm(xz[0:512, :], dzr[:, HD:])).astype(BF16)
+    kc[512:1024, :] = regroup(mm(xq[0:512, :], dzr[:, 0:HD])).astype(BF16)
+    c2 = put(kc, kcr, 7, at(dc=1))
     c2.start()
-    own[0:512, :] = cpre[0, 512:1024, :] * va + cpre[1, 512:1024, :] * vc
+    cb[...] = (cpre[0, 0:512, :] * va + cpre[1, 0:512, :] * vc).astype(BF16)
+    c1 = put(cb, cr, 6, at(dc=1))
+    c1.start()
+    kown[0:512, :] = regroup(mm(xz[512:1024, :], dzr[:, HD:]))
+    kown[512:1024, :] = regroup(mm(xq[512:1024, :], dzr[:, 0:HD]))
+    c2.wait_recv()
+    for k in RING:
+        for p, i, axis in ((0, 9, "dy"), (1, 12, "dz_")):
+            a = slice(p * 512 + k * 64, p * 512 + k * 64 + 64)
+            kb[p, k] = (kown[a, :] + kcr[a, :].astype(F32)).astype(BF16)
+            put(kb.at[p, k], kr.at[p, k], i, at(**{axis: k})).start()
+    own[...] = cpre[0, 512:1024, :] * va + cpre[1, 512:1024, :] * vc
     c1.wait_recv()
-
-    def xsums(p, i):
-        for k in (2, 1, 3):
-            a = slice(p * 512 + k * 128, p * 512 + (k + 1) * 128)
-            xb[p, k] = (own[a, :] + cr[a, :].astype(F32)).astype(BF16)
-            put(xb.at[p, k], xr.at[p, k], i, at(dx=k)).start()
-
-    xsums(0, 8)
-    own[512:1024, :] = mm(xz[512:1024, :], dzr[...])
-    c2.wait_recv()
-    xsums(1, 9)
-
-    whole(gys, gyr, 5, "dy").wait_recv()
-    g = jnp.sum(gyr[...], axis=0)
+    for k in (2, 1, 3):
+        a = slice(k * 128, (k + 1) * 128)
+        xb[k] = (own[a, :] + cr[a, :].astype(F32)).astype(BF16)
+        put(xb.at[k], xr.at[k], 8, at(dx=k)).start()
+
+    whole(gys.at[0], gyr.at[0], 5, "dy").wait_recv()
+    whole(gys.at[1], gyr.at[1], 16, "dz_").wait_recv()
+    g = jnp.concatenate([mine[p] + jnp.sum(gyr[p, 1:8].astype(F32), axis=0) for p in range(2)], axis=1)
     gp = mm(jnp.concatenate([g, jnp.zeros((6, D), F32)], axis=0).astype(BF16), pz[...], NT)
     m2 = jnp.concatenate([mvec[0, 0:1, :], mvec[1, 0:1, :]], axis=0)
     for dc in range(2):
@@ -271,22 +294,17 @@
         dx_o[h] = (r * (dn - xn * mean) + keep * gh).astype(BF16)
         return carry
 
-    lax.fori_loop(0, 2, back, 0)
-
-    def xtotal(p, i):
-        put(xb.at[p, 1:4], xr.at[p, 1:4], i, at(dx=1)).wait_recv()
-        t = own[p * 512 : p * 512 + 128, :] + cr[p * 512 : p * 512 + 128, :].astype(F32)
-        for k in range(1, 4):
-            t = t + xr[p, k].astype(F32)
-        return t
-
-    t0 = xtotal(0, 8)
-    t1 = xtotal(1, 9)
+    lax.fori_loop(0, 1, back, 0)
+
+    whole(xb, xr, 8, "dx").wait_recv()
+    t0 = own[0:128, :] + cr[0:128, :].astype(F32)
+    for k in range(1, 4):
+        t0 = t0 + xr[k].astype(F32)
     put(gm.at[1:8], gmr.at[1:8], 10, at(dc=1)).wait_recv()
     gx = jnp.concatenate([gmr[k, 0:2, :] for k in range(8)], axis=0)
     mx = jnp.concatenate([gmr[k, 2:4, :] for k in range(8)], axis=0)
     so = mm(gx.astype(BF16), mx.astype(BF16), TN)
-    t = jnp.concatenate([t0, t1, so], axis=1)
+    t = jnp.concatenate([t0, so], axis=1)
     fbt[...] = t.astype(BF16)
     for a in RING + (0,):
         for b in RING + (0,):
@@ -295,6 +313,24 @@
                 fb[k] = fbt[2 * k : 2 * k + 2, :]
                 put(fb.at[k], fr.at[k], 11, at(dy=a, dz_=b)).start()
 
+    lax.fori_loop(1, 2, back, 0)
+
+    tk = []
+    for p, i, axis in ((0, 9, "dy"), (1, 12, "dz_")):
+        whole(kb.at[p], kr.at[p], i, axis).wait_recv()
+        a = slice(p * 512, p * 512 + 64)
+        q = kown[a, :] + kcr[a, :].astype(F32)
+        for k in range(1, 8):
+            q = q + kr[p, k].astype(F32)
+        tk.append(q[0:2])
+        for a in (2, 1, 3, 0):
+            for b in RING + (0,):
+                k = a * 8 + b
+                if k:
+                    kf[p, k] = q[2 * k : 2 * k + 2]
+                    other = {"dx": a, ("dy", "dz_")[1 - p]: b}
+                    put(kf.at[p, k], kfr.at[p, k], 13 + p, at(**other)).start()
+
     @pl.when(c == 0)
     def _():
         put(tvb, tvb, 0, at(dc=1)).wait_send()
@@ -308,15 +344,21 @@
     for cp in (g_core, c1, c2):
         cp.wait_send()
     whole(ub, gzr, 3, "dz_", 16).wait_send()
-    whole(gys, gyr, 5, "dy").wait_send()
-    put(xb.at[0, 1:4], xr.at[0, 1:4], 8, at(dx=1)).wait_send()
-    put(xb.at[1, 1:4], xr.at[1, 1:4], 9, at(dx=1)).wait_send()
+    whole(ub.at[128:256], gzr.at[128:256], 15, "dy", 16).wait_send()
+    whole(gys.at[0], gyr.at[0], 5, "dy").wait_send()
+    whole(gys.at[1], gyr.at[1], 16, "dz_").wait_send()
+    whole(xb, xr, 8, "dx").wait_send()
+    whole(kb.at[0], kr.at[0], 9, "dy").wait_send()
+    whole(kb.at[1], kr.at[1], 12, "dz_").wait_send()
     put(gm.at[1:8], gmr.at[1:8], 10, at(dc=1)).wait_send()
 
     put(fb.at[1:64], fr.at[1:64], 11, at(dy=1)).wait()
     f = t[0:2, :] + jnp.sum(fr[1:64].astype(F32), axis=0)
-    gin_o[...] = f[:, 0:512]
-    gout_o[...] = f[:, 512:640]
+    gin_o[:, 0:256] = f[:, 0:256]
+    gout_o[...] = f[:, 256:384]
+    for p, cols in ((1, slice(256, 384)), (0, slice(384, 512))):
+        put(kf.at[p, 1:32], kfr.at[p, 1:32], 13 + p, at(dx=1)).wait()
+        gin_o[:, cols] = tk[p] + jnp.sum(kfr[p, 1:32], axis=0)
 
 
 def finish(dx_v, gin_v, gout_v, dx_o, gin_o, gout_o, sem):
@@ -342,16 +384,18 @@
         scratch_shapes=[
             V((1, 128), I32), V((4, 128), I32), V((256, D), BF16), V((2, L, D), BF16), V((D, 512), BF16), V((HD, D), BF16),
             V((256, HD), F32), V((256, HD), BF16), V((480, HD), BF16), V((8, 4, HD), F32), V((8, 4, HD), F32), V((4, HD), F32),
-            V((128, D), BF16), V((128, D), BF16), V((128, D), F32), V((128, D), BF16), V((128, D), BF16),
-            V((8, 2, D), F32), V((8, 2, D), F32),
-            V((D, D), BF16), V((D, 512), BF16),
+            V((256, 512), BF16), V((256, 512), BF16), V((256, 512), F32), V((256, 512), BF16), V((256, 512), BF16),
+            V((2, 8, 2, 512), BF16), V((2, 8, 2, 512), BF16),
+            V((D, D), BF16), V((D, 512), BF16), V((D, 512), BF16),
             V((2, L, HD), F32), V((2, L, 256), F32), V((2, L, 256), BF16), V((2, L, L), BF16), V((2, L, L), F32),
             V((2, L, 3 * HD), BF16), V((2, L, 256), F32), V((2, L, HD), F32),
             V((512, 512), BF16), V((512, 256), BF16), V((2, 8, HD), F32), V((2, D, 256), F32),
-            V((1024, 256), BF16), V((1024, 256), BF16), V((1024, 256), F32),
-            V((2, 4, 128, 256), BF16), V((2, 4, 128, 256), BF16),
-            V((8, 4, HD), F32), V((8, 4, HD), F32), V((128, 640), BF16), V((64, 2, 640), BF16), V((64, 2, 640), BF16),
-            pltpu.SemaphoreType.DMA((6,)), pltpu.SemaphoreType.DMA((12,)), pltpu.SemaphoreType.DMA((12,)),
+            V((512, 256), BF16), V((512, 256), BF16), V((512, 256), F32),
+            V((1024, HD), BF16), V((1024, HD), BF16), V((1024, HD), F32),
+            V((4, 128, 256), BF16), V((4, 128, 256), BF16), V((2, 8, 64, HD), BF16), V((2, 8, 64, HD), BF16),
+            V((8, 4, HD), F32), V((8, 4, HD), F32), V((128, 384), BF16), V((64, 2, 384), BF16), V((64, 2, 384), BF16),
+            V((2, 32, 2, HD), F32), V((2, 32, 2, HD), F32),
+            pltpu.SemaphoreType.DMA((6,)), pltpu.SemaphoreType.DMA((17,)), pltpu.SemaphoreType.DMA((17,)),
         ],
         compiler_params=pltpu.CompilerParams(
             collective_id=0, has_side_effects=True, vmem_limit_bytes=VMEM

time: 46.8 us -> 43.1 us (0.921)
  Pallas kernels: 46 us -> 42.3 us
    pallas_call x1, Pallas kernels: 45 us -> 41.3 us  [body(): pl.pallas_call(kernel, out_shape=(V((2, L, D), BF16), V((2, 512), F32), V...]
where the time goes in v4:
time: 43.1 us; the launch traced here: 42.9 us
  Pallas kernels  42.3 us (98%)
  between operations  0.64 us (1%)
    pallas_call x1, Pallas kernels, body(): pl.pallas_call(kernel, out_shape=(V((2, L, D), BF16), V((2, 512), F32), V...  41.3 us
    pallas_call x1, Pallas kernels, body(): pl.pallas_call(finish, out_shape=(sd((2, L, D), BF16), sd((2, 512), F32),...  1.02 us

profile of v4, /device:TPU:1, one launch (start us, length us, event | category | flops | bytes accessed | tf_op | source)
XLA Modules:
  0.0 42.9 jit_solution(18259497874008566934)
XLA Ops:
  0.6 41.3 %encoder_backward.1 = (bf16[2,256,1024]{2,1,0:T(8,128)(2,1)S(1)}, f32[2,512]{1,0:T(2,128)S(1)}, f32[2,128]{1,0:T(2,128)S(1)}) custom-call(s32[2]{0:T(128)} %len_s.1, s32[1,128]{1,0:T(1,128)} %cnt_h.1, s32[4,128]{1,0:T(4,128)} %bitcast.2, bf16[256,1024]{1,0:T(8,128)(2,1)} %sg_h.1, bf16[2,256,1024]{2,1,0:T(8,128)(2,1)} %hist_h.1, bf16[1024,512]{1,0:T(8,128)(2,1)} %wi_h.1, ...), custom_call_target="tpu_custom_call" | custom-call | tf_op jit(solution)/shard_map/encoder_backward/pallas_call | solution.py:379
  41.9 1.0 %finish.1 = (bf16[2,256,1024]{2,1,0:T(8,128)(2,1)}, f32[2,512]{1,0:T(2,128)}, f32[2,128]{1,0:T(2,128)}) custom-call(bf16[2,256,1024]{2,1,0:T(8,128)(2,1)S(1)} %get-tuple-element.9.dx_v, f32[2,512]{1,0:T(2,128)S(1)} %get-tuple-element.10.gin_v, f32[2,128]{1,0:T(2,128)S(1)} %get-tuple-element.11.gout_v), custom_call_target="tpu_custom_call" | custom-call | tf_op jit(solution)/shard_map/finish/pallas_call | solution.py:405

commit v5 on v4

--- a/solution.py
+++ b/solution.py
@@ -52,6 +52,16 @@
         a = slice(1, n) if rows is None else slice(rows, rows * n)
         return put(src.at[a], dst.at[a], i, at(**{axis: 1}))
 
+    barrier = pltpu.get_barrier_semaphore()
+    peers = [at(dc=1)] + [at(dy=k) for k in RING] + [at(dz_=k) for k in RING] + [at(dx=k) for k in (2, 1, 3)]
+    for dev in peers:
+        pl.semaphore_signal(barrier, 1, device_id=dev, device_id_type=MESH)
+
+    @pl.when(c == 1)
+    def _():
+        for k in RING:
+            pl.semaphore_signal(barrier, 1, device_id=at(dz_=k, core=0), device_id_type=MESH)
+
     def fetch(i, src, dst):
         cp = pltpu.make_async_copy(src, dst, load.at[i])
         cp.start()
@@ -61,24 +71,13 @@
     for k in range(0, 256, 64):
         pltpu.make_async_copy(sg_h.at[k : k + 64], sg.at[k : k + 64], load.at[2]).start()
     small += [pltpu.make_async_copy(sg_h, sg, load.at[2]), fetch(3, wo_h, wo)]
-
-    barrier = pltpu.get_barrier_semaphore()
-    peers = [at(dc=1)] + [at(dy=k) for k in RING] + [at(dz_=k) for k in RING] + [at(dx=k) for k in (2, 1, 3)]
-    for dev in peers:
-        pl.semaphore_signal(barrier, 1, device_id=dev, device_id_type=MESH)
-
-    @pl.when(c == 1)
-    def _():
-        for k in RING:
-            pl.semaphore_signal(barrier, 1, device_id=at(dz_=k, core=0), device_id_type=MESH)
-
     large = [fetch(4, hist_h, hist), fetch(5, wi_h, wi)]
 
     ri = lax.broadcasted_iota(I32, (256, 1), 0)
     lane = lax.broadcasted_iota(I32, (256, 128), 1)
     samp = lax.broadcasted_iota(I32, (256, 256), 1).astype(F32)
     user = lax.rem(ri, 2).astype(F32)
-    for cp in small:
+    for cp in small[:2]:
         cp.wait()
     cnt = cnt_v[...].astype(F32)
     slots = slot_v[...].astype(F32).astype(BF16)
@@ -96,6 +95,8 @@
         return hit.astype(BF16)
 
     hit = onehot(lax.rem(ri // 4, 8), ri // 32, lax.rem(ri // 2, 2))
+    for cp in small[2:]:
+        cp.wait()
     tv[...] = mm(hit, mm(sg[...], wo[...], NT).astype(BF16))
     tvb[...] = tv[...].astype(BF16)
 
@@ -231,6 +232,9 @@
     v = jnp.where(c == 0, vfin[0:2, :], vfin[2:4, :])
     va = jnp.concatenate([v[0:1], v[0:1]], axis=1)
     vc = jnp.concatenate([v[1:2], v[1:2]], axis=1)
+    cb[...] = (cpre[0, 0:512, :] * va + cpre[1, 0:512, :] * vc).astype(BF16)
+    c1 = put(cb, cr, 6, at(dc=1))
+    c1.start()
     for h in range(2):
         datt = (kgate[h] * v[h : h + 1, :]).astype(BF16)
         ds = (mm(datt, pj[h, :, 0:HD], NT) * dsw[h]).astype(BF16)
@@ -249,9 +253,12 @@
     kc[512:1024, :] = regroup(mm(xq[0:512, :], dzr[:, 0:HD])).astype(BF16)
     c2 = put(kc, kcr, 7, at(dc=1))
     c2.start()
-    cb[...] = (cpre[0, 0:512, :] * va + cpre[1, 0:512, :] * vc).astype(BF16)
-    c1 = put(cb, cr, 6, at(dc=1))
-    c1.start()
+    own[...] = cpre[0, 512:1024, :] * va + cpre[1, 512:1024, :] * vc
+    c1.wait_recv()
+    for k in (2, 1, 3):
+        a = slice(k * 128, (k + 1) * 128)
+        xb[k] = (own[a, :] + cr[a, :].astype(F32)).astype(BF16)
+        put(xb.at[k], xr.at[k], 8, at(dx=k)).start()
     kown[0:512, :] = regroup(mm(xz[512:1024, :], dzr[:, HD:]))
     kown[512:1024, :] = regroup(mm(xq[512:1024, :], dzr[:, 0:HD]))
     c2.wait_recv()
@@ -260,12 +267,6 @@
             a = slice(p * 512 + k * 64, p * 512 + k * 64 + 64)
             kb[p, k] = (kown[a, :] + kcr[a, :].astype(F32)).astype(BF16)
             put(kb.at[p, k], kr.at[p, k], i, at(**{axis: k})).start()
-    own[...] = cpre[0, 512:1024, :] * va + cpre[1, 512:1024, :] * vc
-    c1.wait_recv()
-    for k in (2, 1, 3):
-        a = slice(k * 128, (k + 1) * 128)
-        xb[k] = (own[a, :] + cr[a, :].astype(F32)).astype(BF16)
-        put(xb.at[k], xr.at[k], 8, at(dx=k)).start()
 
     whole(gys.at[0], gyr.at[0], 5, "dy").wait_recv()
     whole(gys.at[1], gyr.at[1], 16, "dz_").wait_recv()

time: 43.1 us -> 42.3 us (0.981)
  Pallas kernels: 42.3 us -> 41.5 us
    pallas_call x1, Pallas kernels: 41.3 us -> 40.5 us  [body(): pl.pallas_call(kernel, out_shape=(V((2, L, D), BF16), V((2, 512), F32), V...]
where the time goes in v5:
time: 42.3 us; the launch traced here: 42.2 us
  Pallas kernels  41.5 us (98%)
  between operations  0.64 us (2%)
    pallas_call x1, Pallas kernels, body(): pl.pallas_call(kernel, out_shape=(V((2, L, D), BF16), V((2, 512), F32), V...  40.5 us
    pallas_call x1, Pallas kernels, body(): pl.pallas_call(finish, out_shape=(sd((2, L, D), BF16), sd((2, 512), F32),...  1.02 us

profile of v5, /device:TPU:1, one launch (start us, length us, event | category | flops | bytes accessed | tf_op | source)
XLA Modules:
  0.0 42.2 jit_solution(318257052293650042)
XLA Ops:
  0.6 40.5 %encoder_backward.1 = (bf16[2,256,1024]{2,1,0:T(8,128)(2,1)S(1)}, f32[2,512]{1,0:T(2,128)S(1)}, f32[2,128]{1,0:T(2,128)S(1)}) custom-call(s32[2]{0:T(128)} %len_s.1, s32[1,128]{1,0:T(1,128)} %cnt_h.1, s32[4,128]{1,0:T(4,128)} %bitcast.2, bf16[256,1024]{1,0:T(8,128)(2,1)} %sg_h.1, bf16[2,256,1024]{2,1,0:T(8,128)(2,1)} %hist_h.1, bf16[1024,512]{1,0:T(8,128)(2,1)} %wi_h.1, ...), custom_call_target="tpu_custom_call" | custom-call | tf_op jit(solution)/shard_map/encoder_backward/pallas_call | solution.py:380
  41.1 1.0 %finish.1 = (bf16[2,256,1024]{2,1,0:T(8,128)(2,1)}, f32[2,512]{1,0:T(2,128)}, f32[2,128]{1,0:T(2,128)}) custom-call(bf16[2,256,1024]{2,1,0:T(8,128)(2,1)S(1)} %get-tuple-element.9.dx_v, f32[2,512]{1,0:T(2,128)S(1)} %get-tuple-element.10.gin_v, f32[2,128]{1,0:T(2,128)S(1)} %get-tuple-element.11.gout_v), custom_call_target="tpu_custom_call" | custom-call | tf_op jit(solution)/shard_map/finish/pallas_call | solution.py:406

commit v6 on v5

--- a/solution.py
+++ b/solution.py
@@ -22,7 +22,7 @@
     len_s, cnt_h, slot_h, sg_h, hist_h, wi_h, wo_h,
     dx_o, gin_o, gout_o,
     cnt_v, slot_v, sg, hist, wi, wo,
-    tv, tvb, vzr, vys, vyr, vfin,
+    tv, tvb, vzr, vys, vyr,
     tb, tr, ua, ub, gzr, gys, gyr,
     pz, xz, xq,
     kgate, pre, preg, wgt, dsw, pj, dsl, rs, dz, dzr, mvec, cpre,
@@ -61,6 +61,11 @@
     def _():
         for k in RING:
             pl.semaphore_signal(barrier, 1, device_id=at(dz_=k, core=0), device_id_type=MESH)
+
+    @pl.when(c == 0)
+    def _():
+        for k in RING:
+            pl.semaphore_signal(barrier, 1, device_id=at(dy=k, core=1), device_id_type=MESH)
 
     def fetch(i, src, dst):
         cp = pltpu.make_async_copy(src, dst, load.at[i])
@@ -104,7 +109,7 @@
         slot = pl.ds(pl.multiple_of((k + 7 * c) * 32, 32), 32)
         return put(tvb.at[32 * k : 32 * k + 32], vzr.at[slot], 0, at(dz_=k, core=1))
 
-    pl.semaphore_wait(barrier, len(peers) + 7 * (1 - c))
+    pl.semaphore_wait(barrier, len(peers) + 7)
     for k in RING:
         vput(k).start()
 
@@ -180,9 +185,13 @@
         for k in range(15):
             s = s + vzr[32 * k : 32 * k + 32, :].astype(F32)
         for k in range(8):
-            vys[k] = s[4 * k : 4 * k + 4]
-        many(vys, vyr, 2, "dy")
-        vyr[0] = s[0:4]
+            vys[0, k] = s[4 * k : 4 * k + 2]
+            vys[1, k] = s[4 * k + 2 : 4 * k + 4]
+        for k in RING:
+            put(vys.at[0, k], vyr.at[k], 4, at(dy=k, core=0)).start()
+            put(vys.at[1, k], vyr.at[k], 2, at(dy=k)).start()
+        put(vys.at[0, 0], vyr.at[0], 4, at(dc=1)).start()
+        vyr[0] = s[2:4]
 
     pr = lax.broadcasted_iota(I32, (512, 1), 0)
     fl = lax.broadcasted_iota(I32, (512, D), 1)
@@ -217,19 +226,15 @@
             gys[p, k] = s1[2 * k : 2 * k + 2]
         many(gys.at[p], gyr.at[p], i, axis)
 
-    v_core = put(vfin, vfin, 4, at(dc=1))
-
     @pl.when(c == 1)
     def _():
-        whole(vys, vyr, 2, "dy").wait_recv()
-        vfin[...] = jnp.sum(vyr[...], axis=0)
-        v_core.start()
+        whole(vys.at[1], vyr, 2, "dy").wait_recv()
 
     @pl.when(c == 0)
     def _():
-        v_core.wait_recv()
-
-    v = jnp.where(c == 0, vfin[0:2, :], vfin[2:4, :])
+        put(vyr, vyr, 4, at(dc=1)).wait_recv()
+
+    v = jnp.sum(vyr[...], axis=0)
     va = jnp.concatenate([v[0:1], v[0:1]], axis=1)
     vc = jnp.concatenate([v[1:2], v[1:2]], axis=1)
     cb[...] = (cpre[0, 0:512, :] * va + cpre[1, 0:512, :] * vc).astype(BF16)
@@ -295,7 +300,6 @@
         dx_o[h] = (r * (dn - xn * mean) + keep * gh).astype(BF16)
         return carry
 
-    lax.fori_loop(0, 1, back, 0)
 
     whole(xb, xr, 8, "dx").wait_recv()
     t0 = own[0:128, :] + cr[0:128, :].astype(F32)
@@ -314,7 +318,6 @@
                 fb[k] = fbt[2 * k : 2 * k + 2, :]
                 put(fb.at[k], fr.at[k], 11, at(dy=a, dz_=b)).start()
 
-    lax.fori_loop(1, 2, back, 0)
 
     tk = []
     for p, i, axis in ((0, 9, "dy"), (1, 12, "dz_")):
@@ -332,6 +335,8 @@
                     other = {"dx": a, ("dy", "dz_")[1 - p]: b}
                     put(kf.at[p, k], kfr.at[p, k], 13 + p, at(**other)).start()
 
+    lax.fori_loop(0, 2, back, 0)
+
     @pl.when(c == 0)
     def _():
         put(tvb, tvb, 0, at(dc=1)).wait_send()
@@ -339,8 +344,8 @@
     @pl.when(c == 1)
     def _():
         put(tvb.at[32:256], tvb.at[32:256], 0, at(dc=1)).wait_send()
-        whole(vys, vyr, 2, "dy").wait_send()
-        v_core.wait_send()
+        whole(vys.at[1], vyr, 2, "dy").wait_send()
+        put(vys.at[0], vyr, 4, at(dc=1)).wait_send()
 
     for cp in (g_core, c1, c2):
         cp.wait_send()
@@ -384,7 +389,7 @@
         out_specs=(vm, vm, vm),
         scratch_shapes=[
             V((1, 128), I32), V((4, 128), I32), V((256, D), BF16), V((2, L, D), BF16), V((D, 512), BF16), V((HD, D), BF16),
-            V((256, HD), F32), V((256, HD), BF16), V((480, HD), BF16), V((8, 4, HD), F32), V((8, 4, HD), F32), V((4, HD), F32),
+            V((256, HD), F32), V((256, HD), BF16), V((480, HD), BF16), V((2, 8, 2, HD), F32), V((8, 2, HD), F32),
             V((256, 512), BF16), V((256, 512), BF16), V((256, 512), F32), V((256, 512), BF16), V((256, 512), BF16),
             V((2, 8, 2, 512), BF16), V((2, 8, 2, 512), BF16),
             V((D, D), BF16), V((D, 512), BF16), V((D, 512), BF16),

time: 42.3 us -> 42.1 us (level)
  no operation moved by 1% of the time
where the time goes in v6:
time: 42.1 us; the launch traced here: 41.9 us
  Pallas kernels  41.3 us (98%)
  between operations  0.64 us (2%)
    pallas_call x1, Pallas kernels, body(): pl.pallas_call(kernel, out_shape=(V((2, L, D), BF16), V((2, 512), F32), V...  40.3 us
    pallas_call x1, Pallas kernels, body(): pl.pallas_call(finish, out_shape=(sd((2, L, D), BF16), sd((2, 512), F32),...  1.02 us

profile of v6, /device:TPU:1, one launch (start us, length us, event | category | flops | bytes accessed | tf_op | source)
XLA Modules:
  0.0 41.9 jit_solution(16761910134562280253)
XLA Ops:
  0.6 40.3 %encoder_backward.1 = (bf16[2,256,1024]{2,1,0:T(8,128)(2,1)S(1)}, f32[2,512]{1,0:T(2,128)S(1)}, f32[2,128]{1,0:T(2,128)S(1)}) custom-call(s32[2]{0:T(128)} %len_s.1, s32[1,128]{1,0:T(1,128)} %cnt_h.1, s32[4,128]{1,0:T(4,128)} %bitcast.2, bf16[256,1024]{1,0:T(8,128)(2,1)} %sg_h.1, bf16[2,256,1024]{2,1,0:T(8,128)(2,1)} %hist_h.1, bf16[1024,512]{1,0:T(8,128)(2,1)} %wi_h.1, ...), custom_call_target="tpu_custom_call" | custom-call | tf_op jit(solution)/shard_map/encoder_backward/pallas_call | solution.py:385
  40.9 1.0 %finish.1 = (bf16[2,256,1024]{2,1,0:T(8,128)(2,1)}, f32[2,512]{1,0:T(2,128)}, f32[2,128]{1,0:T(2,128)}) custom-call(bf16[2,256,1024]{2,1,0:T(8,128)(2,1)S(1)} %get-tuple-element.9.dx_v, f32[2,512]{1,0:T(2,128)S(1)} %get-tuple-element.10.gin_v, f32[2,128]{1,0:T(2,128)S(1)} %get-tuple-element.11.gout_v), custom_call_target="tpu_custom_call" | custom-call | tf_op jit(solution)/shard_map/finish/pallas_call | solution.py:411
